TPU v7x, 512 devices: a whole 4x8x8 slice. The times are simulated.
512 devices in a mesh: dp: 64 (over z, y), mp: 8 (over x, core).
Axes of the slice: x: 4, y: 8, z: 8, core: 2. Of those that a mesh axis runs over, the one named last changes fastest.
Arguments:
- hidden_states: bfloat16 [65536, 8192], P('dp', 'mp'), may hold values from -6 to 6
- key_grad: bfloat16 [65536, 1024], P('dp'), may hold values from -0.23925781 to 0.23925781
- error_buffer: bfloat16 [64, 8192, 1024], P('dp', 'mp'), may hold values from -6 to 6
- q_init: float32 [1024, 32], replicated, may hold values from -6 to 6
Outputs:
- q_factor: float32 [1024, 32], P('mp')
All inputs are finite; a program needn't handle non-finite values.
Results may differ from a plain program's by a relative error of at most 0.0003.
Values sent between devices are 32-bit elements; how exact they have to be, the bound alone decides.
No kernel may reach another device: no remote copies, remote signals or barrier semaphores. Data moves between devices by JAX's collectives and lax.ppermute only.
A program may use at most 64 MiB of HBM per device.

v0:
```python
import jax
import jax.numpy as jnp
from jax import lax
from jax.sharding import PartitionSpec as P


def shards(hidden_states, key_grad, error_buffer, q_init):
    replicas = lax.axis_size("dp")
    width_devices = lax.axis_size("mp")
    own_rows = hidden_states.shape[1]
    gradient = lax.dot_general(
        hidden_states, key_grad, (((0,), (0,)), ((), ())), preferred_element_type=jnp.float32
    )
    combined = gradient + error_buffer[0].astype(jnp.float32)
    local_p = jnp.dot(combined, q_init, precision=lax.Precision.HIGHEST)
    padded = jnp.zeros((own_rows * width_devices, local_p.shape[1]), jnp.float32)
    padded = lax.dynamic_update_slice_in_dim(padded, local_p, lax.axis_index("mp") * own_rows, 0)
    full_p = lax.psum(padded, ("dp", "mp")) / replicas
    gram = jnp.dot(full_p.T, full_p, precision=lax.Precision.HIGHEST)
    p_factor = lax.dynamic_slice_in_dim(full_p, lax.axis_index("mp") * own_rows, own_rows, 0)
    lower = jnp.linalg.cholesky(gram)
    basis = jax.scipy.linalg.solve_triangular(lower, p_factor.T, lower=True).T
    local_q = lax.dot_general(
        combined, basis, (((0,), (0,)), ((), ())), precision=lax.Precision.HIGHEST
    )
    total_q = lax.psum(local_q, ("dp", "mp")) / replicas
    share = local_q.shape[0] // width_devices
    return lax.dynamic_slice_in_dim(total_q, lax.axis_index("mp") * share, share, 0)


def solution(mesh):
    in_specs = (P("dp", "mp"), P("dp", None), P("dp", "mp", None), P())
    out_specs = P("mp", None)
    return jax.shard_map(shards, mesh=mesh, in_specs=in_specs, out_specs=out_specs, check_vma=False)
```

profile of v0, /device:TPU:1, one launch (start us, length us, event | category | flops | bytes accessed | tf_op | source)
XLA Modules:
  0.0 581.1 jit_solution(3006163311110742460)
XLA Ops:
  6.5 0.0 copy-start
  6.5 0.0 all-reduce.3.cloned.1.call-start
  6.5 1.6 copy-done
  8.1 0.0 copy-start.2
  8.1 0.0 copy-start.5
  8.1 4.2 fusion.12
  12.3 0.0 copy-start.1
  12.3 0.1 broadcast_in_dim.5
  12.4 1.9 copy-done.1
  14.2 0.0 copy-done.2
  14.3 0.0 copy-done.5
  14.3 4.0 fusion.4
  18.3 0.0 copy-start.4
  18.3 1.0 copy-done.4
  19.3 0.0 all-reduce.3.cloned.1.call-update
  19.3 0.0 all-reduce.5.cloned.1.call-start
  19.4 278.1 %all-reduce.3.cloned.1.call-done = f32[8192,32]{0,1:T(8,128)} async-done(((f32[8192,32]{0,1:T(8,128)}), f32[8192,32]{0,1:T(8,128)}) %all-reduce.3.cloned.1.call-update) | async-done | bytes 1048592 | tf_op jit(solution)/shard_map/psum | solution.py:18
  297.5 2.6 fusion.11
  300.1 0.1 copy.5
  300.2 2.9 cholesky.16
  303.1 0.6 compare_reduce_fusion
  303.8 0.7 fusion.7
  304.4 2.4 custom-call.7
  306.9 0.0 copy-start.3
  306.9 1.5 broadcast_multiply_fusion
  308.3 0.3 fusion.5
  308.7 0.1 copy-done.3
  308.8 5.7 fusion
  314.5 0.0 all-reduce.5.cloned.1.call-update
  314.5 258.4 %all-reduce.5.cloned.1.call-done = f32[1024,32]{0,1:T(8,128)} async-done(((f32[1024,32]{0,1:T(8,128)}), f32[1024,32]{0,1:T(8,128)}) %all-reduce.5.cloned.1.call-update) | async-done | bytes 131088 | tf_op jit(solution)/shard_map/psum | solution.py:26
  572.9 1.3 dynamic-slice_multiply_fusion
  (2 shorter events, 0.0 us)
Async XLA Ops:
  6.5 1.6 copy-start
  6.5 291.0 %all-reduce.3.cloned.1.call-start = ((), (), s32[]{:S(2)}) async-start(), calls=%async_computation | async-start | bytes 2097152 | tf_op jit(solution)/shard_map/psum | solution.py:18
  8.1 6.1 %copy-start.2 = (bf16[1,1024,1024]{2,1,0:T(8,128)(2,1)S(1)}, bf16[1,1024,1024]{2,1,0:T(8,128)(2,1)}, u32[]{:S(2)}) copy-start(bf16[1,1024,1024]{2,1,0:T(8,128)(2,1)} %param.6) | copy-start | bytes 6291460
  8.1 6.1 %copy-start.5 = (f32[1024,32]{0,1:T(8,128)S(1)}, f32[1024,32]{0,1:T(8,128)}, u32[]{:S(2)}) copy-start(f32[1024,32]{0,1:T(8,128)} %param.7) | copy-start | bytes 393220
  12.3 1.9 copy-start.1
  18.3 1.0 copy-start.4
  19.3 553.6 %all-reduce.5.cloned.1.call-start = ((), (), s32[]{:S(2)}) async-start(), calls=%async_computation.1 | async-start | bytes 262144 | tf_op jit(solution)/shard_map/psum | solution.py:26
  306.9 1.9 copy-start.3
Sparse Core Ops, SparseCore 0:
  19.4 278.0 all-reduce.2
  314.6 258.2 all-reduce.4
where the time goes:
time: 581 us
  waiting for transfers between devices  537 us (92%)
  matrix products  16.7 us (3%)
  between operations  13.5 us (2%)
  other arithmetic  9.48 us (2%)
    psum x1, waiting for transfers between devices, shards(): full_p = lax.psum(padded, ('dp', 'mp')) / replicas  278 us
    psum x1, waiting for transfers between devices, shards(): total_q = lax.psum(local_q, ('dp', 'mp')) / replicas  258 us
  transfers between devices with their start and end apart: 2, of which 2 were waited for; matrix products, arithmetic and copies ran while one was open for 0% of the time, Pallas kernels for 0%

commit v1 on v0

v1 whole, which is shorter than its diff:
```python
import jax
import jax.numpy as jnp
from jax import lax
from jax.sharding import Mesh, PartitionSpec as P

DP = ("zh", "zl", "yh", "yl")
MP = ("x", "core")
NEAR = ("zl", "yl", "x", "core")


def pieces(value):
    high = lax.reduce_precision(value, 8, 7)
    return jnp.concatenate([high, value - high], 0).astype(jnp.bfloat16)


def thin(left, right, contract):
    rank = left.shape[0]
    out = lax.dot_general(pieces(left), right, (((1,), (contract,)), ((), ())), preferred_element_type=jnp.float32)
    return out[:rank] + out[rank:]


def left_partial(hidden, key_grad, error, q_init):
    q_t = q_init.T
    u_t = thin(q_t, key_grad, 1)
    p_t = thin(u_t, hidden, 0) + thin(q_t, error, 1)
    return p_t.reshape(8, 4, 8, 128).transpose(2, 0, 1, 3).reshape(64, 4, 128)


def right_partial(hidden, key_grad, error, p_blocks):
    p_t = p_blocks.reshape(8, 8, 4, 128).transpose(1, 2, 0, 3).reshape(32, 1024)
    v_t = thin(p_t, hidden, 1)
    q_t = thin(v_t, key_grad, 0) + thin(p_t, error, 0)
    gram = jnp.dot(p_t, p_t.T, precision=lax.Precision.HIGHEST)
    blocks = q_t.reshape(4, 8, 8, 128).transpose(0, 2, 1, 3).reshape(32, 8, 128)
    packed = gram.reshape(4, 8, 32).transpose(1, 0, 2).reshape(1, 8, 128)
    return jnp.concatenate([blocks, jnp.broadcast_to(packed, (32, 8, 128))], 1)


def finish(blocks, packed):
    gram = packed.reshape(8, 4, 32).transpose(1, 0, 2).reshape(32, 32)
    q_t = blocks.reshape(4, 2, 4, 2, 8, 128).sum((0, 2)).reshape(32, 128)
    lower = jnp.linalg.cholesky(gram)
    return jax.scipy.linalg.solve_triangular(lower, q_t, lower=True).T


def shards(hidden, key_grad, error, q_init):
    part = left_partial(hidden, key_grad, error[0], q_init)
    part = lax.all_to_all(part, DP, 0, 0, tiled=True)
    own = part.sum(0) / 64
    p_blocks = lax.all_to_all(jnp.broadcast_to(own, (64, 4, 128)), DP, 0, 0, tiled=True)
    part = right_partial(hidden, key_grad, error[0], p_blocks)
    part = lax.all_to_all(part, NEAR, 0, 0, tiled=True)
    near = part.sum(0)
    packed = near[8:] * 0.25
    blocks = lax.all_to_all(jnp.broadcast_to(near[:8] / 64, (64, 8, 128)), DP, 0, 0, tiled=True)
    return finish(blocks, packed)


def solution(mesh):
    fine = Mesh(mesh.devices.reshape(4, 2, 4, 2, 4, 2), DP + MP)
    in_specs = (P(DP, MP), P(DP, None), P(DP, MP, None), P())
    return jax.shard_map(shards, mesh=fine, in_specs=in_specs, out_specs=P(MP, None), check_vma=False)
```

time: 581 us -> 89.8 us (0.15)
  the two profiles are of different devices: /device:TPU:1 before, /device:TPU:8 now
where the time goes in v1:
time: 89.8 us; the launch traced here: 89.5 us
  blocking collectives  58 us (65%)
  other arithmetic  8.06 us (9%)
  matrix products  8 us (9%)
  waiting for transfers between devices  8 us (9%)
  starting transfers between devices  5.85 us (7%)
  local copies, waits for them, and re-layouts  1.31 us (1%)
    all_to_all x1, blocking collectives, shards(): part = lax.all_to_all(part, DP, 0, 0, tiled=True)  28.3 us
    all_to_all x1, blocking collectives, shards(): lax.all_to_all(jnp.broadcast_to(own, (64, 4, 128)), DP, 0, 0, tiled=True)  16.6 us
    all_to_all x1, blocking collectives, shards(): part = lax.all_to_all(part, NEAR, 0, 0, tiled=True)  13.1 us
    all_to_all x1, waiting for transfers between devices, shards(): lax.all_to_all(jnp.broadcast_to(near[:8] / 64, (64, 8, 128)), DP, 0, 0, t...  8 us
    dot_general x6, matrix products, thin(): lax.dot_general(pieces(left), right, (((1,), (contract,)), ((), ())), pre...  6.97 us
    all_to_all x1, starting transfers between devices, shards(): lax.all_to_all(jnp.broadcast_to(near[:8] / 64, (64, 8, 128)), DP, 0, 0, t...  5.85 us
    another operation x3, other arithmetic, finish(): lower = jnp.linalg.cholesky(gram)  3.59 us
    another operation x2, other arithmetic, finish(): return jax.scipy.linalg.solve_triangular(lower, q_t, lower=True).T  3.09 us
  transfers between devices with their start and end apart: 1, of which 1 were waited for; matrix products, arithmetic and copies ran while one was open for 7% of the time, Pallas kernels for 0%

profile of v1, /device:TPU:8, one launch (start us, length us, event | category | flops | bytes accessed | tf_op | source)
XLA Modules:
  0.0 89.5 jit_solution(3215849914978683482)
XLA Ops:
  0.0 0.0 copy-start
  0.0 0.0 copy-start.1
  0.0 1.1 %reduce-precision_convert_fusion.3 = (bf16[32,1024]{1,0:T(8,128)(2,1)S(1)}, bf16[32,1024]{1,0:T(8,128)(2,1)S(1)}) fusion(f32[1024,32]{0,1:T(8,128)} %param.7), kind=kLoop, calls=%fused_computation.13 | loop fusion | flops 131072 | bytes 262144 | tf_op jit(solution)/shard_map/convert.6
  1.1 2.4 %fusion.20 = f32[64,1024]{1,0:T(8,128)S(1)} fusion(bf16[1024,1024]{1,0:T(8,128)(2,1)} %param.5, bf16[32,1024]{1,0:T(8,128)(2,1)S(1)} %get-tuple-element.12, bf16[32,1024]{1,0:T(8,128)(2,1)S(1)} %get-tuple-element.11), kind=kOutput, calls=%fused_computation.40 | convolution fusion | flops 134479872 | bytes 2490368 | tf_op jit(solution)/shard_map/dot_general | solution.py:18
  3.5 0.0 copy-done.1
  3.6 0.8 fusion.2
  4.3 0.0 copy-done
  4.3 0.5 fusion.11
  4.9 0.1 copy.38
  5.0 0.1 copy.21
  5.1 28.3 %all_to_all.20 = f32[64,4,128]{2,1,0:T(4,128)S(1)} all-to-all(f32[64,4,128]{2,1,0:T(4,128)S(1)} %copy.21), channel_id=1, replica_groups=mesh['zh'=4,'zl'=2,'yh'=4,'yl'=2,'x'=4,'core'=2] {'zh','zl','yh','yl'}, dimensions={0} | all-to-all | bytes 262144 | tf_op jit(solution)/shard_map/all_to_all | solution.py:48
  33.3 0.1 reduce_sum.27
  33.4 0.0 copy-start.2
  33.5 16.6 %all_to_all.21 = f32[64,4,128]{2,1,0:T(4,128)S(1)} all-to-all(f32[64,4,128]{2,1,0:T(4,128)S(1)} %broadcast_in_dim.15), channel_id=1, replica_groups=mesh['zh'=4,'zl'=2,'yh'=4,'yl'=2,'x'=4,'core'=2] {'zh','zl','yh','yl'}, dimensions={0} | all-to-all | bytes 262144 | tf_op jit(solution)/shard_map/all_to_all | solution.py:50
  50.2 0.8 fusion.19
  50.9 0.0 copy-done.2
  51.0 0.5 fusion
  51.5 0.2 convolution_bitcast_fusion
  51.8 0.1 broadcast_in_dim.16
  51.9 2.1 %fusion.15 = f32[64,1024]{1,0:T(8,128)S(1)} fusion(bf16[1024,1024]{1,0:T(8,128)(2,1)} %param.5, bf16[32,1024]{1,0:T(8,128)(2,1)S(1)} %get-tuple-element.6, bf16[32,1024]{1,0:T(8,128)(2,1)S(1)} %get-tuple-element.5), kind=kOutput, calls=%fused_computation.33 | convolution fusion | flops 134479872 | bytes 2490368 | tf_op jit(solution)/shard_map/dot_general | solution.py:18
  54.0 13.1 %all_to_all.22 = f32[32,16,128]{2,1,0:T(8,128)S(1)} all-to-all(f32[32,16,128]{2,1,0:T(8,128)S(1)} %pad_maximum_fusion), channel_id=1, replica_groups=mesh['zh'=4,'zl'=2,'yh'=4,'yl'=2,'x'=4,'core'=2] {'zl','yl','x','core'}, dimensions={0} | all-to-all | bytes 524288 | tf_op jit(solution)/shard_map/all_to_all | solution.py:52
  67.2 0.1 reshape.53
  67.3 0.1 copy.27
  67.3 0.7 broadcast_in_dim.18
  68.1 5.9 %all-to-all-start.3 = ((f32[64,8,128]{2,1,0:T(8,128)}), f32[64,8,128]{2,1,0:T(8,128)S(1)}, u32[]{:S(2)}, u32[]{:S(2)}) async-start(f32[64,8,128]{2,1,0:T(8,128)} %broadcast_in_dim.18), calls=%async_computation.3 | async-start | bytes 524288 | tf_op jit(solution)/shard_map/all_to_all | solution.py:55
  73.9 2.9 %cholesky.16 = f32[32,32]{1,0:T(8,128)S(1)} custom-call(f32[32,32]{1,0:T(8,128)S(1)} %fusion.24), custom_call_target="Cholesky" | custom-call | tf_op jit(solution)/shard_map/jit(cholesky)/cholesky | solution.py:42
  76.9 0.6 compare_reduce_fusion
  77.5 0.7 fusion.21
  78.2 2.4 %custom-call.7 = f32[1,32,32]{1,2,0:T(8,128)S(1)} custom-call(f32[1,32,32]{2,1,0:T(8,128)S(1)} %fusion.21), custom_call_target="InvertDiagBlocksLowerTriangular" | custom-call | tf_op jit(solution)/shard_map/jit(_solve_triangular)/triangular_solve | solution.py:43
  80.6 8.0 %all-to-all-done.3 = f32[64,8,128]{2,1,0:T(8,128)S(1)} async-done(((f32[64,8,128]{2,1,0:T(8,128)}), f32[64,8,128]{2,1,0:T(8,128)S(1)}, u32[]{:S(2)}, u32[]{:S(2)}) %all-to-all-start.3) | async-done | bytes 262176 | tf_op jit(solution)/shard_map/all_to_all | solution.py:55
  88.6 0.8 fusion.22
  (21 shorter events, 0.4 us)
Async XLA Ops:
  0.0 4.3 %copy-start = (bf16[1024,1024]{1,0:T(8,128)(2,1)S(1)}, bf16[1024,1024]{1,0:T(8,128)(2,1)}, u32[]{:S(2)}) copy-start(bf16[1024,1024]{1,0:T(8,128)(2,1)} %param.4) | copy-start | bytes 6291460
  0.0 3.5 %copy-start.1 = (bf16[1,1024,1024]{2,1,0:T(8,128)(2,1)S(1)}, bf16[1,1024,1024]{2,1,0:T(8,128)(2,1)}, u32[]{:S(2)}) copy-start(bf16[1,1024,1024]{2,1,0:T(8,128)(2,1)} %param.6) | copy-start | bytes 6291460
  33.4 17.5 %copy-start.2 = (bf16[1,1024,1024]{2,1,0:T(8,128)(2,1)S(1)}, bf16[1,1024,1024]{2,1,0:T(8,128)(2,1)}, u32[]{:S(2)}) copy-start(bf16[1,1024,1024]{2,1,0:T(8,128)(2,1)} %param.6) | copy-start | bytes 6291460
  68.1 20.6 %all-to-all-start.3 = ((f32[64,8,128]{2,1,0:T(8,128)}), f32[64,8,128]{2,1,0:T(8,128)S(1)}, u32[]{:S(2)}, u32[]{:S(2)}) async-start(f32[64,8,128]{2,1,0:T(8,128)} %broadcast_in_dim.18), calls=%async_computation.3 | async-start | bytes 524288 | tf_op jit(solution)/shard_map/all_to_all | solution.py:55

commit v2 on v0

v2 whole, which is shorter than its diff:
```python
import jax
import jax.experimental.pallas as pl
import jax.experimental.pallas.tpu as pltpu
import jax.numpy as jnp
from jax import lax
from jax.sharding import Mesh, PartitionSpec as P

DP = ("z2", "z1", "z0", "y2", "y1", "y0")
MP = ("x", "core")
LEFT_NEAR = ("z1", "z0", "y2", "y1", "y0")
RIGHT_NEAR = ("z0", "y0", "x", "core")

F32, BF16 = jnp.float32, jnp.bfloat16
RANK, WIDTH, HALF = 32, 1024, 512
NN = (((1,), (0,)), ((), ()))
NT = (((1,), (1,)), ((), ()))
VMEM = pl.BlockSpec(memory_space=pltpu.VMEM)
HBM = pl.BlockSpec(memory_space=pltpu.HBM)
PARAMS = pltpu.CompilerParams(vmem_limit_bytes=24 << 20)


def in_vmem(*arrays):
    return [pltpu.with_memory_space_constraint(a, pltpu.VMEM) for a in arrays]


def in_hbm(*arrays):
    return [pltpu.with_memory_space_constraint(a, pltpu.HBM) for a in arrays]


def dot(a, b, dims):
    return lax.dot_general(a, b, dims, preferred_element_type=F32)


def pieces(value):
    high = value.astype(BF16)
    return jnp.concatenate([high, (value - high.astype(F32)).astype(BF16)], 0)


def fold(product):
    return product[:RANK] + product[RANK:]


def left_kernel(q_hbm, key_hbm, error_hbm, hidden_hbm, out, key, error, hidden, q, acc, sems):
    first = pltpu.make_async_copy(q_hbm, q, sems.at[0])
    first.start()
    copies = []
    for source, target in ((key_hbm, key), (error_hbm, error), (hidden_hbm, hidden)):
        for at in range(0, WIDTH, HALF):
            rows = pl.ds(at, HALF)
            copies.append(pltpu.make_async_copy(source.at[rows, :], target.at[rows, :], sems.at[1 + len(copies)]))
            copies[-1].start()
    first.wait()
    q2 = pieces(q[...])
    inner = []
    for i in range(2):
        copies[i].wait()
        inner.append(pieces(fold(dot(q2, key[i * HALF:(i + 1) * HALF, :], NT))))
    for i in range(2):
        copies[2 + i].wait()
        acc[:, i * HALF:(i + 1) * HALF] = fold(dot(q2, error[i * HALF:(i + 1) * HALF, :], NT))
    copies[4].wait()
    total = dot(inner[0], hidden[:HALF, :], NN)
    copies[5].wait()
    total = fold(total + dot(inner[1], hidden[HALF:, :], NN)) + acc[...]
    for k in range(32):
        out[k] = total[8 * (k % 4):8 * (k % 4) + 8, 128 * (k // 4):128 * (k // 4) + 128]


def left_partial(q_t, key, error, hidden):
    big = pltpu.VMEM((WIDTH, WIDTH), BF16)
    thin = pltpu.VMEM((RANK, WIDTH), F32)
    return pl.pallas_call(
        left_kernel,
        out_shape=(pltpu.VMEM((32, 8, 128), F32), big, big, big),
        in_specs=[HBM] * 4,
        out_specs=(VMEM,) * 4,
        scratch_shapes=[thin, thin, pltpu.SemaphoreType.DMA((7,))],
        compiler_params=PARAMS,
        name="left_partial",
    )(*in_hbm(q_t, key, error, hidden))


def left_sum_kernel(parts, out):
    total = jnp.sum(parts[...], 0)
    for k in range(64):
        out[k] = total


def left_sum(parts):
    return pl.pallas_call(
        left_sum_kernel,
        out_shape=pltpu.VMEM((64, 8, 128), F32),
        in_specs=[VMEM],
        out_specs=VMEM,
        compiler_params=PARAMS,
        name="left_sum",
    )(*in_vmem(parts))


def right_kernel(tiles, key, error, hidden, out):
    columns = [
        jnp.concatenate([tiles[4 * b + a] + tiles[32 + 4 * b + a] for a in range(4)], 0) for b in range(8)
    ]
    p2 = pieces(jnp.concatenate(columns, 1) * (1 / 64))
    inner = pieces(fold(dot(p2, hidden[...], NT)))
    total = fold(dot(p2, error[...], NN) + dot(inner, key[...], NN)) * (1 / 64)
    gram = fold(dot(p2, p2, NT))
    gram = (gram[:, :RANK] + gram[:, RANK:]) * 0.25
    packed = jnp.concatenate([gram[8 * s:8 * s + 8] for s in range(4)], 1)
    for k in range(32):
        s, m = k // 8, k % 8
        out[k, :8] = total[8 * s:8 * s + 8, 128 * m:128 * m + 128]
        out[k, 8:] = packed


def right_partial(tiles, key, error, hidden):
    return pl.pallas_call(
        right_kernel,
        out_shape=pltpu.VMEM((32, 16, 128), F32),
        in_specs=[VMEM] * 4,
        out_specs=VMEM,
        compiler_params=PARAMS,
        name="right_partial",
    )(*in_vmem(tiles, key, error, hidden))


def right_sum_kernel(parts, out, gram):
    total = jnp.sum(parts[...], 0)
    for k in range(64):
        out[k] = total[:8]
    for s in range(4):
        gram[8 * s:8 * s + 8, :] = total[8:, RANK * s:RANK * s + RANK]


def right_sum(parts):
    return pl.pallas_call(
        right_sum_kernel,
        out_shape=(pltpu.VMEM((64, 8, 128), F32), pltpu.VMEM((RANK, RANK), F32)),
        in_specs=[VMEM],
        out_specs=(VMEM, VMEM),
        compiler_params=PARAMS,
        name="right_sum",
    )(*in_vmem(parts))


def finish_kernel(tiles, inverse, out):
    rows = []
    for s in range(4):
        total = tiles[s // 2 * 8 + s % 2]
        for r in range(1, 16):
            total = total + tiles[r // 4 * 16 + s // 2 * 8 + r % 4 * 2 + s % 2]
        rows.append(total)
    out[...] = jnp.dot(inverse[...], jnp.concatenate(rows, 0), precision=lax.Precision.HIGHEST, preferred_element_type=F32)


def finish(tiles, inverse):
    return pl.pallas_call(
        finish_kernel,
        out_shape=jax.ShapeDtypeStruct((RANK, 128), F32),
        in_specs=[VMEM, VMEM],
        out_specs=VMEM,
        compiler_params=PARAMS,
        name="finish",
    )(*in_vmem(tiles, inverse))


def shards(hidden, key, error, q_init):
    error = error[0]
    part, key, error, hidden = left_partial(q_init.T, key, error, hidden)
    part = lax.all_to_all(part, LEFT_NEAR, 0, 0, tiled=True)
    tiles = lax.all_to_all(left_sum(part), DP, 0, 0, tiled=True)
    part = lax.all_to_all(right_partial(tiles, key, error, hidden), RIGHT_NEAR, 0, 0, tiled=True)
    tiles, gram = right_sum(part)
    tiles = lax.all_to_all(tiles, DP, 0, 0, tiled=True)
    lower = jnp.linalg.cholesky(gram)
    inverse = jax.scipy.linalg.solve_triangular(lower, jnp.eye(RANK, dtype=F32), lower=True)
    return finish(tiles, inverse).T


def solution(mesh):
    fine = Mesh(mesh.devices.reshape(2, 2, 2, 2, 2, 2, 4, 2), DP + MP)
    in_specs = (P(DP, MP), P(DP, None), P(DP, MP, None), P())
    return jax.shard_map(shards, mesh=fine, in_specs=in_specs, out_specs=P(MP, None), check_vma=False)
```

time: 581 us -> 86.5 us (0.15)
  the two profiles are of different devices: /device:TPU:1 before, /device:TPU:8 now
where the time goes in v2:
time: 86.5 us; the launch traced here: 86.2 us
  blocking collectives  58.8 us (68%)
  waiting for transfers between devices  7.61 us (9%)
  other arithmetic  6.69 us (8%)
  Pallas kernels  6.63 us (8%)
  starting transfers between devices  6.17 us (7%)
    all_to_all x1, blocking collectives, shards(): part = lax.all_to_all(part, LEFT_NEAR, 0, 0, tiled=True)  22.9 us
    all_to_all x1, blocking collectives, shards(): tiles = lax.all_to_all(left_sum(part), DP, 0, 0, tiled=True)  22.8 us
    all_to_all x1, blocking collectives, shards(): lax.all_to_all(right_partial(tiles, key, error, hidden), RIGHT_NEAR, 0, 0...  13.1 us
    all_to_all x1, waiting for transfers between devices, shards(): tiles = lax.all_to_all(tiles, DP, 0, 0, tiled=True)  7.61 us
    all_to_all x1, starting transfers between devices, shards(): tiles = lax.all_to_all(tiles, DP, 0, 0, tiled=True)  6.17 us
    another operation x3, other arithmetic, shards(): lower = jnp.linalg.cholesky(gram)  3.6 us
    pallas_call x1, Pallas kernels, left_partial(): pl.pallas_call(left_kernel, out_shape=(pltpu.VMEM((32, 8, 128), F32), big...  3.47 us
    another operation x2, other arithmetic, shards(): jax.scipy.linalg.solve_triangular(lower, jnp.eye(RANK, dtype=F32), lower=...  3.09 us
  transfers between devices with their start and end apart: 1, of which 1 were waited for; matrix products, arithmetic and copies ran while one was open for 8% of the time, Pallas kernels for 0%

profile of v2, /device:TPU:8, one launch (start us, length us, event | category | flops | bytes accessed | tf_op | source)
XLA Modules:
  0.0 86.2 jit_solution(2737073993331779422)
XLA Ops:
  0.0 3.5 %left_partial.1 = (f32[32,8,128]{2,1,0:T(8,128)S(1)}, bf16[1024,1024]{1,0:T(8,128)(2,1)S(1)}, bf16[1024,1024]{1,0:T(8,128)(2,1)S(1)}, bf16[1024,1024]{1,0:T(8,128)(2,1)S(1)}) custom-call(f32[32,1024]{1,0:T(8,128)} %bitcast.13, bf16[1024,1024]{1,0:T(8,128)(2,1)} %key_hbm.1, bf16[1024,1024]{1,0:T(8,128)(2,1)} %bitcast.12, bf16[1024,1024]{1,0:T(8,128)(2,1)} %hidden_hbm.1), custom_call_target="tpu_custom_call" | custom-call | tf_op jit(solution)/shard_map/left_partial/pallas_call | solution.py:72
  3.5 22.9 %all_to_all.20.parts = f32[32,8,128]{2,1,0:T(8,128)S(1)} all-to-all(f32[32,8,128]{2,1,0:T(8,128)S(1)} %get-tuple-element.11), channel_id=1, replica_groups=mesh['z2'=2,'z1'=2,'z0'=2,'y2'=2,'y1'=2,'y0'=2,'x'=4,'core'=2] {'z1','z0..., dimensions={0} | all-to-all | bytes 262144 | tf_op jit(solution)/shard_map/all_to_all | solution.py:170
  26.4 0.1 left_sum.1
  26.4 22.8 %all_to_all.21.tiles = f32[64,8,128]{2,1,0:T(8,128)S(1)} all-to-all(f32[64,8,128]{2,1,0:T(8,128)S(1)} %left_sum.1), channel_id=1, replica_groups=mesh['z2'=2,'z1'=2,'z0'=2,'y2'=2,'y1'=2,'y0'=2,'x'=4,'core'=2] {'z2','z1..., dimensions={0} | all-to-all | bytes 524288 | tf_op jit(solution)/shard_map/all_to_all | solution.py:171
  49.2 1.6 %right_partial.1 = f32[32,16,128]{2,1,0:T(8,128)S(1)} custom-call(f32[64,8,128]{2,1,0:T(8,128)S(1)} %all_to_all.21.tiles, bf16[1024,1024]{1,0:T(8,128)(2,1)S(1)} %get-tuple-element.12.key, bf16[1024,1024]{1,0:T(8,128)(2,1)S(1)} %get-tuple-element.13.error, bf16[1024,1024]{1,0:T(8,128)(2,1)S(1)} %get-tuple-element.14.hidden), custom_call_target="tpu_custom_call" | custom-call | tf_op jit(solution)/shard_map/right_partial/pallas_call | solution.py:117
  50.8 13.1 %all_to_all.22.parts = f32[32,16,128]{2,1,0:T(8,128)S(1)} all-to-all(f32[32,16,128]{2,1,0:T(8,128)S(1)} %right_partial.1), channel_id=1, replica_groups=mesh['z2'=2,'z1'=2,'z0'=2,'y2'=2,'y1'=2,'y0'=2,'x'=4,'core'=2] {'z0','y0..., dimensions={0} | all-to-all | bytes 524288 | tf_op jit(solution)/shard_map/all_to_all | solution.py:172
  63.9 0.7 right_sum.1
  64.7 6.2 %all-to-all-start.3 = ((f32[64,8,128]{2,1,0:T(8,128)}), f32[64,8,128]{2,1,0:T(8,128)S(1)}, u32[]{:S(2)}, u32[]{:S(2)}) async-start(f32[64,8,128]{2,1,0:T(8,128)} %get-tuple-element.15), calls=%async_computation.3 | async-start | bytes 524288 | tf_op jit(solution)/shard_map/all_to_all | solution.py:174
  70.8 0.1 copy.5
  70.9 2.9 %cholesky.17 = f32[32,32]{1,0:T(8,128)S(1)} custom-call(f32[32,32]{1,0:T(8,128)S(1)} %fusion.3), custom_call_target="Cholesky" | custom-call | tf_op jit(solution)/shard_map/jit(cholesky)/cholesky | solution.py:175
  73.9 0.6 compare_reduce_fusion
  74.5 0.7 fusion
  75.2 2.4 %custom-call.7 = f32[1,32,32]{1,2,0:T(8,128)S(1)} custom-call(f32[1,32,32]{2,1,0:T(8,128)S(1)} %fusion), custom_call_target="InvertDiagBlocksLowerTriangular" | custom-call | tf_op jit(solution)/shard_map/jit(_solve_triangular)/triangular_solve | solution.py:176
  77.6 0.2 fusion.1.inverse
  77.8 7.6 %all-to-all-done.3.tiles = f32[64,8,128]{2,1,0:T(8,128)S(1)} async-done(((f32[64,8,128]{2,1,0:T(8,128)}), f32[64,8,128]{2,1,0:T(8,128)S(1)}, u32[]{:S(2)}, u32[]{:S(2)}) %all-to-all-start.3) | async-done | bytes 262176 | tf_op jit(solution)/shard_map/all_to_all | solution.py:174
  85.4 0.8 finish.1
  (2 shorter events, 0.0 us)
Async XLA Ops:
  64.7 20.8 %all-to-all-start.3 = ((f32[64,8,128]{2,1,0:T(8,128)}), f32[64,8,128]{2,1,0:T(8,128)S(1)}, u32[]{:S(2)}, u32[]{:S(2)}) async-start(f32[64,8,128]{2,1,0:T(8,128)} %get-tuple-element.15), calls=%async_computation.3 | async-start | bytes 524288 | tf_op jit(solution)/shard_map/all_to_all | solution.py:174

commit v3 on v2

--- a/solution.py
+++ b/solution.py
@@ -32,12 +32,15 @@
 
 
 def pieces(value):
-    high = value.astype(BF16)
-    return jnp.concatenate([high, (value - high.astype(F32)).astype(BF16)], 0)
+    parts = []
+    for _ in range(3):
+        parts.append(value.astype(BF16))
+        value = value - parts[-1].astype(F32)
+    return jnp.concatenate(parts, 0)
 
 
 def fold(product):
-    return product[:RANK] + product[RANK:]
+    return product[:RANK] + product[RANK:2 * RANK] + product[2 * RANK:]
 
 
 def left_kernel(q_hbm, key_hbm, error_hbm, hidden_hbm, out, key, error, hidden, q, acc, sems):
@@ -105,7 +108,7 @@
     inner = pieces(fold(dot(p2, hidden[...], NT)))
     total = fold(dot(p2, error[...], NN) + dot(inner, key[...], NN)) * (1 / 64)
     gram = fold(dot(p2, p2, NT))
-    gram = (gram[:, :RANK] + gram[:, RANK:]) * 0.25
+    gram = (gram[:, :RANK] + gram[:, RANK:2 * RANK] + gram[:, 2 * RANK:]) * 0.25
     packed = jnp.concatenate([gram[8 * s:8 * s + 8] for s in range(4)], 1)
     for k in range(32):
         s, m = k // 8, k % 8
@@ -129,13 +132,13 @@
     for k in range(64):
         out[k] = total[:8]
     for s in range(4):
-        gram[8 * s:8 * s + 8, :] = total[8:, RANK * s:RANK * s + RANK]
+        gram[8 * s:8 * s + 8, :] = pltpu.roll(total[8:], 128 - RANK * s, 1) if s else total[8:]
 
 
 def right_sum(parts):
     return pl.pallas_call(
         right_sum_kernel,
-        out_shape=(pltpu.VMEM((64, 8, 128), F32), pltpu.VMEM((RANK, RANK), F32)),
+        out_shape=(pltpu.VMEM((64, 8, 128), F32), pltpu.VMEM((RANK, 128), F32)),
         in_specs=[VMEM],
         out_specs=(VMEM, VMEM),
         compiler_params=PARAMS,
@@ -143,17 +146,53 @@
     )(*in_vmem(parts))
 
 
-def finish_kernel(tiles, inverse, out):
+def along_lanes(tile, j):
+    return jnp.broadcast_to(tile[:, j:j + 1], (8, 128))
+
+
+def along_rows(tile, j):
+    return jnp.broadcast_to(tile[j:j + 1, :], (8, 128))
+
+
+def finish_kernel(tiles, gram, out):
     rows = []
     for s in range(4):
         total = tiles[s // 2 * 8 + s % 2]
         for r in range(1, 16):
             total = total + tiles[r // 4 * 16 + s // 2 * 8 + r % 4 * 2 + s % 2]
         rows.append(total)
-    out[...] = jnp.dot(inverse[...], jnp.concatenate(rows, 0), precision=lax.Precision.HIGHEST, preferred_element_type=F32)
-
-
-def finish(tiles, inverse):
+    rest = [gram[8 * s:8 * s + 8, :] for s in range(4)]
+    row = lax.broadcasted_iota(jnp.int32, (8, 128), 0)
+    for b in range(4):
+        column = {s: [along_lanes(rest[s], 8 * b + q) for q in range(8)] for s in range(b, 4)}
+        block = [[along_rows(column[b][q], p) for q in range(p + 1)] for p in range(8)]
+        pivot_rest = [along_rows(rest[b], p) for p in range(8)]
+        pivot_rows = [along_rows(rows[b], p) for p in range(8)]
+        inverse = []
+        for q in range(8):
+            inverse.append(1.0 / block[q][q])
+            for p in range(q + 1, 8):
+                factor = block[p][q] * inverse[q]
+                pivot_rest[p] = pivot_rest[p] - factor * pivot_rest[q]
+                pivot_rows[p] = pivot_rows[p] - factor * pivot_rows[q]
+                for t in range(q + 1, p + 1):
+                    block[p][t] = block[p][t] - factor * block[t][q]
+        for s in range(b, 4):
+            for q in range(8):
+                factor = column[s][q] * inverse[q]
+                if s == b:
+                    factor = jnp.where(row > q, factor, 0.0)
+                for t in range(q + 1, 8):
+                    column[s][t] = column[s][t] - factor * block[t][q]
+                rest[s] = rest[s] - factor * pivot_rest[q]
+                rows[s] = rows[s] - factor * pivot_rows[q]
+        scale = lax.rsqrt(block[0][0])
+        for q in range(1, 8):
+            scale = jnp.where(row == q, lax.rsqrt(block[q][q]), scale)
+        out[8 * b:8 * b + 8, :] = rows[b] * scale
+
+
+def finish(tiles, gram):
     return pl.pallas_call(
         finish_kernel,
         out_shape=jax.ShapeDtypeStruct((RANK, 128), F32),
@@ -161,7 +200,7 @@
         out_specs=VMEM,
         compiler_params=PARAMS,
         name="finish",
-    )(*in_vmem(tiles, inverse))
+    )(*in_vmem(tiles, gram))
 
 
 def shards(hidden, key, error, q_init):
@@ -171,10 +210,7 @@
     tiles = lax.all_to_all(left_sum(part), DP, 0, 0, tiled=True)
     part = lax.all_to_all(right_partial(tiles, key, error, hidden), RIGHT_NEAR, 0, 0, tiled=True)
     tiles, gram = right_sum(part)
-    tiles = lax.all_to_all(tiles, DP, 0, 0, tiled=True)
-    lower = jnp.linalg.cholesky(gram)
-    inverse = jax.scipy.linalg.solve_triangular(lower, jnp.eye(RANK, dtype=F32), lower=True)
-    return finish(tiles, inverse).T
+    return finish(lax.all_to_all(tiles, DP, 0, 0, tiled=True), gram).T
 
 
 def solution(mesh):

time: 86.5 us -> 86.4 us (level)
  blocking collectives: 58.8 us -> 79.3 us
  waiting for transfers between devices: 7.61 us -> 0 us
  other arithmetic: 6.69 us -> 0 us
  starting transfers between devices: 6.17 us -> 0 us
    all_to_all x0 -> x1, blocking collectives: none -> 20.6 us  [shards(): return finish(lax.all_to_all(tiles, DP, 0, 0, tiled=True), gram).T]
    all_to_all x1 -> x0, waiting for transfers between devices: 7.61 us -> none  [shards(): tiles = lax.all_to_all(tiles, DP, 0, 0, tiled=True)]
    another operation x5 -> x0, other arithmetic: 6.68 us -> none  [the longest x3 3.6 us: shards(): lower = jnp.linalg.cholesky(gram)]
    all_to_all x1 -> x0, starting transfers between devices: 6.17 us -> none  [shards(): tiles = lax.all_to_all(tiles, DP, 0, 0, tiled=True)]
  transfers between devices with their start and end apart: 1 -> 0, of which waited for: 1 -> 0; matrix products, arithmetic and copies ran while one was open for 8% -> 0% of each run, Pallas kernels for 0% -> 0%
where the time goes in v3:
time: 86.4 us; the launch traced here: 86.2 us
  blocking collectives  79.3 us (92%)
  Pallas kernels  6.83 us (8%)
    all_to_all x1, blocking collectives, shards(): part = lax.all_to_all(part, LEFT_NEAR, 0, 0, tiled=True)  22.9 us
    all_to_all x1, blocking collectives, shards(): tiles = lax.all_to_all(left_sum(part), DP, 0, 0, tiled=True)  22.8 us
    all_to_all x1, blocking collectives, shards(): return finish(lax.all_to_all(tiles, DP, 0, 0, tiled=True), gram).T  20.6 us
    all_to_all x1, blocking collectives, shards(): lax.all_to_all(right_partial(tiles, key, error, hidden), RIGHT_NEAR, 0, 0...  13.1 us
    pallas_call x1, Pallas kernels, left_partial(): pl.pallas_call(left_kernel, out_shape=(pltpu.VMEM((32, 8, 128), F32), big...  3.51 us
    pallas_call x1, Pallas kernels, right_partial(): pl.pallas_call(right_kernel, out_shape=pltpu.VMEM((32, 16, 128), F32), in...  1.75 us

profile of v3, /device:TPU:8, one launch (start us, length us, event | category | flops | bytes accessed | tf_op | source)
XLA Modules:
  0.0 86.2 jit_solution(18050626629714231882)
XLA Ops:
  0.0 3.5 %left_partial.1 = (f32[32,8,128]{2,1,0:T(8,128)S(1)}, bf16[1024,1024]{1,0:T(8,128)(2,1)S(1)}, bf16[1024,1024]{1,0:T(8,128)(2,1)S(1)}, bf16[1024,1024]{1,0:T(8,128)(2,1)S(1)}) custom-call(f32[32,1024]{1,0:T(8,128)} %bitcast.4, bf16[1024,1024]{1,0:T(8,128)(2,1)} %key_hbm.1, bf16[1024,1024]{1,0:T(8,128)(2,1)} %bitcast.3, bf16[1024,1024]{1,0:T(8,128)(2,1)} %hidden_hbm.1), custom_call_target="tpu_custom_call" | custom-call | tf_op jit(solution)/shard_map/left_partial/pallas_call | solution.py:75
  3.5 22.9 %all_to_all.20.parts = f32[32,8,128]{2,1,0:T(8,128)S(1)} all-to-all(f32[32,8,128]{2,1,0:T(8,128)S(1)} %get-tuple-element.11), channel_id=1, replica_groups=mesh['z2'=2,'z1'=2,'z0'=2,'y2'=2,'y1'=2,'y0'=2,'x'=4,'core'=2] {'z1','z0..., dimensions={0} | all-to-all | bytes 262144 | tf_op jit(solution)/shard_map/all_to_all | solution.py:209
  26.4 0.1 left_sum.1
  26.5 22.8 %all_to_all.21.tiles = f32[64,8,128]{2,1,0:T(8,128)S(1)} all-to-all(f32[64,8,128]{2,1,0:T(8,128)S(1)} %left_sum.1), channel_id=1, replica_groups=mesh['z2'=2,'z1'=2,'z0'=2,'y2'=2,'y1'=2,'y0'=2,'x'=4,'core'=2] {'z2','z1..., dimensions={0} | all-to-all | bytes 524288 | tf_op jit(solution)/shard_map/all_to_all | solution.py:210
  49.2 1.7 %right_partial.1 = f32[32,16,128]{2,1,0:T(8,128)S(1)} custom-call(f32[64,8,128]{2,1,0:T(8,128)S(1)} %all_to_all.21.tiles, bf16[1024,1024]{1,0:T(8,128)(2,1)S(1)} %get-tuple-element.12.key, bf16[1024,1024]{1,0:T(8,128)(2,1)S(1)} %get-tuple-element.13.error, bf16[1024,1024]{1,0:T(8,128)(2,1)S(1)} %get-tuple-element.14.hidden), custom_call_target="tpu_custom_call" | custom-call | tf_op jit(solution)/shard_map/right_partial/pallas_call | solution.py:120
  51.0 13.1 %all_to_all.22.parts = f32[32,16,128]{2,1,0:T(8,128)S(1)} all-to-all(f32[32,16,128]{2,1,0:T(8,128)S(1)} %right_partial.1), channel_id=1, replica_groups=mesh['z2'=2,'z1'=2,'z0'=2,'y2'=2,'y1'=2,'y0'=2,'x'=4,'core'=2] {'z0','y0..., dimensions={0} | all-to-all | bytes 524288 | tf_op jit(solution)/shard_map/all_to_all | solution.py:211
  64.1 0.1 right_sum.1
  64.2 20.6 %all_to_all.23.tiles = f32[64,8,128]{2,1,0:T(8,128)S(1)} all-to-all(f32[64,8,128]{2,1,0:T(8,128)S(1)} %get-tuple-element.15), channel_id=1, replica_groups=mesh['z2'=2,'z1'=2,'z0'=2,'y2'=2,'y1'=2,'y0'=2,'x'=4,'core'=2] {'z2','z1..., dimensions={0} | all-to-all | bytes 524288 | tf_op jit(solution)/shard_map/all_to_all | solution.py:213
  84.8 1.4 %finish.1 = f32[32,128]{1,0:T(8,128)} custom-call(f32[64,8,128]{2,1,0:T(8,128)S(1)} %all_to_all.23.tiles, f32[32,128]{1,0:T(8,128)S(1)} %get-tuple-element.16.gram), custom_call_target="tpu_custom_call" | custom-call | tf_op jit(solution)/shard_map/finish/pallas_call | solution.py:196

commit v4 on v3

--- a/solution.py
+++ b/solution.py
@@ -7,7 +7,6 @@
 
 DP = ("z2", "z1", "z0", "y2", "y1", "y0")
 MP = ("x", "core")
-LEFT_NEAR = ("z1", "z0", "y2", "y1", "y0")
 RIGHT_NEAR = ("z0", "y0", "x", "core")
 
 F32, BF16 = jnp.float32, jnp.bfloat16
@@ -85,14 +84,15 @@
 
 def left_sum_kernel(parts, out):
     total = jnp.sum(parts[...], 0)
-    for k in range(64):
+    total = total + pltpu.roll(total, 4, 0)
+    for k in range(32):
         out[k] = total
 
 
 def left_sum(parts):
     return pl.pallas_call(
         left_sum_kernel,
-        out_shape=pltpu.VMEM((64, 8, 128), F32),
+        out_shape=pltpu.VMEM((32, 8, 128), F32),
         in_specs=[VMEM],
         out_specs=VMEM,
         compiler_params=PARAMS,
@@ -102,7 +102,7 @@
 
 def right_kernel(tiles, key, error, hidden, out):
     columns = [
-        jnp.concatenate([tiles[4 * b + a] + tiles[32 + 4 * b + a] for a in range(4)], 0) for b in range(8)
+        jnp.concatenate([tiles[4 * b + a] for a in range(4)], 0) for b in range(8)
     ]
     p2 = pieces(jnp.concatenate(columns, 1) * (1 / 64))
     inner = pieces(fold(dot(p2, hidden[...], NT)))
@@ -203,11 +203,14 @@
     )(*in_vmem(tiles, gram))
 
 
+def halves_over_dp(tiles):
+    return lax.all_to_all(tiles.reshape(64, 4, 128), DP, 0, 0, tiled=True).reshape(32, 8, 128)
+
+
 def shards(hidden, key, error, q_init):
     error = error[0]
     part, key, error, hidden = left_partial(q_init.T, key, error, hidden)
-    part = lax.all_to_all(part, LEFT_NEAR, 0, 0, tiled=True)
-    tiles = lax.all_to_all(left_sum(part), DP, 0, 0, tiled=True)
+    tiles = halves_over_dp(left_sum(halves_over_dp(part)))
     part = lax.all_to_all(right_partial(tiles, key, error, hidden), RIGHT_NEAR, 0, 0, tiled=True)
     tiles, gram = right_sum(part)
     return finish(lax.all_to_all(tiles, DP, 0, 0, tiled=True), gram).T

time: 86.4 us -> 85.2 us (0.986)
  blocking collectives: 79.3 us -> 78.1 us
    all_to_all x2, blocking collectives: 45.7 us -> 44.8 us  [halves_over_dp(): lax.all_to_all(tiles.reshape(64, 4, 128), DP, 0, 0, tiled=True)]
where the time goes in v4:
time: 85.2 us; the launch traced here: 85 us
  blocking collectives  78.1 us (92%)
  Pallas kernels  6.83 us (8%)
    all_to_all x2, blocking collectives, halves_over_dp(): lax.all_to_all(tiles.reshape(64, 4, 128), DP, 0, 0, tiled=True)  44.8 us
    all_to_all x1, blocking collectives, shards(): return finish(lax.all_to_all(tiles, DP, 0, 0, tiled=True), gram).T  20.2 us
    all_to_all x1, blocking collectives, shards(): lax.all_to_all(right_partial(tiles, key, error, hidden), RIGHT_NEAR, 0, 0...  13.1 us
    pallas_call x1, Pallas kernels, left_partial(): pl.pallas_call(left_kernel, out_shape=(pltpu.VMEM((32, 8, 128), F32), big...  3.51 us
    pallas_call x1, Pallas kernels, right_partial(): pl.pallas_call(right_kernel, out_shape=pltpu.VMEM((32, 16, 128), F32), in...  1.75 us

profile of v4, /device:TPU:8, one launch (start us, length us, event | category | flops | bytes accessed | tf_op | source)
XLA Modules:
  0.0 85.0 jit_solution(4561421843416944073)
XLA Ops:
  0.0 3.5 %left_partial.1 = (f32[32,8,128]{2,1,0:T(8,128)S(1)}, bf16[1024,1024]{1,0:T(8,128)(2,1)S(1)}, bf16[1024,1024]{1,0:T(8,128)(2,1)S(1)}, bf16[1024,1024]{1,0:T(8,128)(2,1)S(1)}) custom-call(f32[32,1024]{1,0:T(8,128)} %bitcast.12, bf16[1024,1024]{1,0:T(8,128)(2,1)} %key_hbm.1, bf16[1024,1024]{1,0:T(8,128)(2,1)} %bitcast.11, bf16[1024,1024]{1,0:T(8,128)(2,1)} %hidden_hbm.1), custom_call_target="tpu_custom_call" | custom-call | tf_op jit(solution)/shard_map/left_partial/pallas_call | solution.py:74
  3.5 28.3 %all_to_all.20 = f32[64,4,128]{2,1,0:T(4,128)S(1)} all-to-all(f32[64,4,128]{2,1,0:T(4,128)S(1)} %bitcast.10), channel_id=1, replica_groups=mesh['z2'=2,'z1'=2,'z0'=2,'y2'=2,'y1'=2,'y0'=2,'x'=4,'core'=2] {'z2','z1..., dimensions={0} | all-to-all | bytes 262144 | tf_op jit(solution)/shard_map/all_to_all | solution.py:207
  31.8 16.5 %all_to_all.21 = f32[64,4,128]{2,1,0:T(4,128)S(1)} all-to-all(f32[64,4,128]{2,1,0:T(4,128)S(1)} %bitcast.9), channel_id=1, replica_groups=mesh['z2'=2,'z1'=2,'z0'=2,'y2'=2,'y1'=2,'y0'=2,'x'=4,'core'=2] {'z2','z1..., dimensions={0} | all-to-all | bytes 262144 | tf_op jit(solution)/shard_map/all_to_all | solution.py:207
  48.4 1.7 %right_partial.1 = f32[32,16,128]{2,1,0:T(8,128)S(1)} custom-call(f32[32,8,128]{2,1,0:T(8,128)S(1)} %bitcast.7, bf16[1024,1024]{1,0:T(8,128)(2,1)S(1)} %get-tuple-element.12.key, bf16[1024,1024]{1,0:T(8,128)(2,1)S(1)} %get-tuple-element.13.error, bf16[1024,1024]{1,0:T(8,128)(2,1)S(1)} %get-tuple-element.14.hidden), custom_call_target="tpu_custom_call" | custom-call | tf_op jit(solution)/shard_map/right_partial/pallas_call | solution.py:120
  50.1 13.1 %all_to_all.22.parts = f32[32,16,128]{2,1,0:T(8,128)S(1)} all-to-all(f32[32,16,128]{2,1,0:T(8,128)S(1)} %right_partial.1), channel_id=1, replica_groups=mesh['z2'=2,'z1'=2,'z0'=2,'y2'=2,'y1'=2,'y0'=2,'x'=4,'core'=2] {'z0','y0..., dimensions={0} | all-to-all | bytes 524288 | tf_op jit(solution)/shard_map/all_to_all | solution.py:214
  63.2 0.1 right_sum.1
  63.3 20.2 %all_to_all.23.tiles = f32[64,8,128]{2,1,0:T(8,128)S(1)} all-to-all(f32[64,8,128]{2,1,0:T(8,128)S(1)} %get-tuple-element.15), channel_id=1, replica_groups=mesh['z2'=2,'z1'=2,'z0'=2,'y2'=2,'y1'=2,'y0'=2,'x'=4,'core'=2] {'z2','z1..., dimensions={0} | all-to-all | bytes 524288 | tf_op jit(solution)/shard_map/all_to_all | solution.py:216
  83.6 1.4 %finish.1 = f32[32,128]{1,0:T(8,128)} custom-call(f32[64,8,128]{2,1,0:T(8,128)S(1)} %all_to_all.23.tiles, f32[32,128]{1,0:T(8,128)S(1)} %get-tuple-element.16.gram), custom_call_target="tpu_custom_call" | custom-call | tf_op jit(solution)/shard_map/finish/pallas_call | solution.py:196
  (1 shorter events, 0.0 us)

commit v5 on v4

--- a/solution.py
+++ b/solution.py
@@ -7,10 +7,12 @@
 
 DP = ("z2", "z1", "z0", "y2", "y1", "y0")
 MP = ("x", "core")
-RIGHT_NEAR = ("z0", "y0", "x", "core")
+STEP_DP = ("y0", "z0", "y1", "z1", "y2", "z2")
+NEAR = ("x", "core", "z0", "y0")
 
 F32, BF16 = jnp.float32, jnp.bfloat16
 RANK, WIDTH, HALF = 32, 1024, 512
+ROWS = 10
 NN = (((1,), (0,)), ((), ()))
 NT = (((1,), (1,)), ((), ()))
 VMEM = pl.BlockSpec(memory_space=pltpu.VMEM)
@@ -100,39 +102,50 @@
     )(*in_vmem(parts))
 
 
-def right_kernel(tiles, key, error, hidden, out):
+def right_kernel(tiles, key, error, hidden, out, gram):
     columns = [
         jnp.concatenate([tiles[4 * b + a] for a in range(4)], 0) for b in range(8)
     ]
-    p2 = pieces(jnp.concatenate(columns, 1) * (1 / 64))
-    inner = pieces(fold(dot(p2, hidden[...], NT)))
-    total = fold(dot(p2, error[...], NN) + dot(inner, key[...], NN)) * (1 / 64)
-    gram = fold(dot(p2, p2, NT))
-    gram = (gram[:, :RANK] + gram[:, RANK:2 * RANK] + gram[:, 2 * RANK:]) * 0.25
-    packed = jnp.concatenate([gram[8 * s:8 * s + 8] for s in range(4)], 1)
-    for k in range(32):
-        s, m = k // 8, k % 8
-        out[k, :8] = total[8 * s:8 * s + 8, 128 * m:128 * m + 128]
-        out[k, 8:] = packed
+    p3 = pieces(jnp.concatenate(columns, 1) * (1 / 64))
+    inner = pieces(fold(dot(p3, hidden[...], NT)))
+    total = fold(dot(p3, error[...], NN) + dot(inner, key[...], NN)) * (1 / 64)
+    square = fold(dot(p3, p3, NT))
+    gram[...] = square[:, :RANK] + square[:, RANK:2 * RANK] + square[:, 2 * RANK:]
+    quarter = 2 * lax.axis_index("z0") + lax.axis_index("y0")
+    own = gram[pl.ds(pl.multiple_of(8 * quarter, 8), 8), :]
+    packed = jnp.concatenate([own[2 * i:2 * i + 2] for i in range(4)], 1)
+    for m in range(8):
+        for s in range(4):
+            at = ROWS * (4 * m + s)
+            out[at:at + 8, :] = total[8 * s:8 * s + 8, 128 * m:128 * m + 128]
+            out[at + 8:at + ROWS, :] = packed
 
 
 def right_partial(tiles, key, error, hidden):
     return pl.pallas_call(
         right_kernel,
-        out_shape=pltpu.VMEM((32, 16, 128), F32),
+        out_shape=pltpu.VMEM((32 * ROWS, 128), F32),
         in_specs=[VMEM] * 4,
         out_specs=VMEM,
+        scratch_shapes=[pltpu.VMEM((RANK, RANK), F32)],
         compiler_params=PARAMS,
         name="right_partial",
     )(*in_vmem(tiles, key, error, hidden))
 
 
 def right_sum_kernel(parts, out, gram):
-    total = jnp.sum(parts[...], 0)
+    total = parts[:8, :]
+    for k in range(1, 32):
+        total = total + parts[ROWS * k:ROWS * k + 8, :]
     for k in range(64):
-        out[k] = total[:8]
+        out[k] = total
     for s in range(4):
-        gram[8 * s:8 * s + 8, :] = pltpu.roll(total[8:], 128 - RANK * s, 1) if s else total[8:]
+        packed = parts[ROWS * s + 8:ROWS * s + ROWS, :]
+        for m in range(1, 8):
+            at = ROWS * (4 * m + s)
+            packed = packed + parts[at + 8:at + ROWS, :]
+        for i in range(4):
+            gram[8 * s + 2 * i:8 * s + 2 * i + 2, :RANK] = packed[:, RANK * i:RANK * i + RANK]
 
 
 def right_sum(parts):
@@ -155,12 +168,7 @@
 
 
 def finish_kernel(tiles, gram, out):
-    rows = []
-    for s in range(4):
-        total = tiles[s // 2 * 8 + s % 2]
-        for r in range(1, 16):
-            total = total + tiles[r // 4 * 16 + s // 2 * 8 + r % 4 * 2 + s % 2]
-        rows.append(total)
+    rows = [jnp.sum(tiles[16 * s:16 * s + 16], 0) for s in (0, 2, 1, 3)]
     rest = [gram[8 * s:8 * s + 8, :] for s in range(4)]
     row = lax.broadcasted_iota(jnp.int32, (8, 128), 0)
     for b in range(4):
@@ -204,16 +212,17 @@
 
 
 def halves_over_dp(tiles):
-    return lax.all_to_all(tiles.reshape(64, 4, 128), DP, 0, 0, tiled=True).reshape(32, 8, 128)
+    return lax.all_to_all(tiles.reshape(64, 4, 128), STEP_DP, 0, 0, tiled=True).reshape(32, 8, 128)
 
 
 def shards(hidden, key, error, q_init):
     error = error[0]
     part, key, error, hidden = left_partial(q_init.T, key, error, hidden)
     tiles = halves_over_dp(left_sum(halves_over_dp(part)))
-    part = lax.all_to_all(right_partial(tiles, key, error, hidden), RIGHT_NEAR, 0, 0, tiled=True)
+    part = right_partial(tiles, key, error, hidden).reshape(-1, 2, 128)
+    part = lax.all_to_all(part, NEAR, 0, 0, tiled=True).reshape(-1, 128)
     tiles, gram = right_sum(part)
-    return finish(lax.all_to_all(tiles, DP, 0, 0, tiled=True), gram).T
+    return finish(lax.all_to_all(tiles, STEP_DP, 0, 0, tiled=True), gram).T
 
 
 def solution(mesh):

time: 85.2 us -> 82.9 us (0.973)
  blocking collectives: 78.1 us -> 75.9 us
    all_to_all x4, blocking collectives: 78.1 us -> 75.9 us  [the longest x2 44 us: halves_over_dp(): lax.all_to_all(tiles.reshape(64, 4, 128), STEP_DP, 0, 0, tiled=True)]
where the time goes in v5:
time: 82.9 us; the launch traced here: 82.7 us
  blocking collectives  75.9 us (92%)
  Pallas kernels  6.82 us (8%)
    all_to_all x2, blocking collectives, halves_over_dp(): lax.all_to_all(tiles.reshape(64, 4, 128), STEP_DP, 0, 0, tiled=True)  44 us
    all_to_all x1, blocking collectives, shards(): return finish(lax.all_to_all(tiles, STEP_DP, 0, 0, tiled=True), gram).T  19.8 us
    all_to_all x1, blocking collectives, shards(): part = lax.all_to_all(part, NEAR, 0, 0, tiled=True).reshape(-1, 128)  12.1 us
    pallas_call x1, Pallas kernels, left_partial(): pl.pallas_call(left_kernel, out_shape=(pltpu.VMEM((32, 8, 128), F32), big...  3.51 us
    pallas_call x1, Pallas kernels, right_partial(): pl.pallas_call(right_kernel, out_shape=pltpu.VMEM((32 * ROWS, 128), F32),...  1.75 us

profile of v5, /device:TPU:8, one launch (start us, length us, event | category | flops | bytes accessed | tf_op | source)
XLA Modules:
  0.0 82.7 jit_solution(16587376356016945519)
XLA Ops:
  0.0 3.5 %left_partial.1 = (f32[32,8,128]{2,1,0:T(8,128)S(1)}, bf16[1024,1024]{1,0:T(8,128)(2,1)S(1)}, bf16[1024,1024]{1,0:T(8,128)(2,1)S(1)}, bf16[1024,1024]{1,0:T(8,128)(2,1)S(1)}) custom-call(f32[32,1024]{1,0:T(8,128)} %bitcast.16, bf16[1024,1024]{1,0:T(8,128)(2,1)} %key_hbm.1, bf16[1024,1024]{1,0:T(8,128)(2,1)} %bitcast.15, bf16[1024,1024]{1,0:T(8,128)(2,1)} %hidden_hbm.1), custom_call_target="tpu_custom_call" | custom-call | tf_op jit(solution)/shard_map/left_partial/pallas_call | solution.py:76
  3.5 28.2 %all_to_all.20 = f32[64,4,128]{2,1,0:T(4,128)S(1)} all-to-all(f32[64,4,128]{2,1,0:T(4,128)S(1)} %bitcast.14), channel_id=1, replica_groups=mesh['z2'=2,'z1'=2,'z0'=2,'y2'=2,'y1'=2,'y0'=2,'x'=4,'core'=2] {'y0','z0..., dimensions={0} | all-to-all | bytes 262144 | tf_op jit(solution)/shard_map/all_to_all | solution.py:215
  31.7 15.8 %all_to_all.21 = f32[64,4,128]{2,1,0:T(4,128)S(1)} all-to-all(f32[64,4,128]{2,1,0:T(4,128)S(1)} %bitcast.13), channel_id=1, replica_groups=mesh['z2'=2,'z1'=2,'z0'=2,'y2'=2,'y1'=2,'y0'=2,'x'=4,'core'=2] {'y0','z0..., dimensions={0} | all-to-all | bytes 262144 | tf_op jit(solution)/shard_map/all_to_all | solution.py:215
  47.5 1.8 %right_partial.1 = f32[320,128]{1,0:T(8,128)S(1)} custom-call(f32[32,8,128]{2,1,0:T(8,128)S(1)} %bitcast.11, bf16[1024,1024]{1,0:T(8,128)(2,1)S(1)} %get-tuple-element.12.key, bf16[1024,1024]{1,0:T(8,128)(2,1)S(1)} %get-tuple-element.13.error, bf16[1024,1024]{1,0:T(8,128)(2,1)S(1)} %get-tuple-element.14.hidden), custom_call_target="tpu_custom_call" | custom-call | tf_op jit(solution)/shard_map/right_partial/pallas_call | solution.py:125
  49.3 12.1 %all_to_all.22 = f32[160,2,128]{2,1,0:T(2,128)S(1)} all-to-all(f32[160,2,128]{2,1,0:T(2,128)S(1)} %bitcast.9), channel_id=1, replica_groups=mesh['z2'=2,'z1'=2,'z0'=2,'y2'=2,'y1'=2,'y0'=2,'x'=4,'core'=2] {'x','cor..., dimensions={0} | all-to-all | bytes 327680 | tf_op jit(solution)/shard_map/all_to_all | solution.py:223
  61.4 0.1 right_sum.1
  61.5 19.8 %all_to_all.23.tiles = f32[64,8,128]{2,1,0:T(8,128)S(1)} all-to-all(f32[64,8,128]{2,1,0:T(8,128)S(1)} %get-tuple-element.15), channel_id=1, replica_groups=mesh['z2'=2,'z1'=2,'z0'=2,'y2'=2,'y1'=2,'y0'=2,'x'=4,'core'=2] {'y0','z0..., dimensions={0} | all-to-all | bytes 524288 | tf_op jit(solution)/shard_map/all_to_all | solution.py:225
  81.3 1.4 %finish.1 = f32[32,128]{1,0:T(8,128)} custom-call(f32[64,8,128]{2,1,0:T(8,128)S(1)} %all_to_all.23.tiles, f32[32,128]{1,0:T(8,128)S(1)} %get-tuple-element.16.gram), custom_call_target="tpu_custom_call" | custom-call | tf_op jit(solution)/shard_map/finish/pallas_call | solution.py:204
  (1 shorter events, 0.0 us)

commit v6 on v5

--- a/solution.py
+++ b/solution.py
@@ -62,10 +62,9 @@
     for i in range(2):
         copies[2 + i].wait()
         acc[:, i * HALF:(i + 1) * HALF] = fold(dot(q2, error[i * HALF:(i + 1) * HALF, :], NT))
-    copies[4].wait()
-    total = dot(inner[0], hidden[:HALF, :], NN)
-    copies[5].wait()
-    total = fold(total + dot(inner[1], hidden[HALF:, :], NN)) + acc[...]
+    for copy in copies[4:]:
+        copy.wait()
+    total = fold(dot(jnp.concatenate(inner, 1), hidden[...], NN)) + acc[...]
     for k in range(32):
         out[k] = total[8 * (k % 4):8 * (k % 4) + 8, 128 * (k // 4):128 * (k // 4) + 128]
 
@@ -107,13 +106,13 @@
         jnp.concatenate([tiles[4 * b + a] for a in range(4)], 0) for b in range(8)
     ]
     p3 = pieces(jnp.concatenate(columns, 1) * (1 / 64))
-    inner = pieces(fold(dot(p3, hidden[...], NT)))
-    total = fold(dot(p3, error[...], NN) + dot(inner, key[...], NN)) * (1 / 64)
     square = fold(dot(p3, p3, NT))
     gram[...] = square[:, :RANK] + square[:, RANK:2 * RANK] + square[:, 2 * RANK:]
     quarter = 2 * lax.axis_index("z0") + lax.axis_index("y0")
     own = gram[pl.ds(pl.multiple_of(8 * quarter, 8), 8), :]
     packed = jnp.concatenate([own[2 * i:2 * i + 2] for i in range(4)], 1)
+    inner = pieces(fold(dot(p3, hidden[...], NT)))
+    total = (fold(dot(p3, error[...], NN)) + fold(dot(inner, key[...], NN))) * (1 / 64)
     for m in range(8):
         for s in range(4):
             at = ROWS * (4 * m + s)

time: 82.9 us -> 82.5 us (level)
  no operation moved by 1% of the time
where the time goes in v6:
time: 82.5 us; the launch traced here: 82.3 us
  blocking collectives  75.9 us (92%)
  Pallas kernels  6.4 us (8%)
    all_to_all x2, blocking collectives, halves_over_dp(): lax.all_to_all(tiles.reshape(64, 4, 128), STEP_DP, 0, 0, tiled=True)  44 us
    all_to_all x1, blocking collectives, shards(): return finish(lax.all_to_all(tiles, STEP_DP, 0, 0, tiled=True), gram).T  19.8 us
    all_to_all x1, blocking collectives, shards(): part = lax.all_to_all(part, NEAR, 0, 0, tiled=True).reshape(-1, 128)  12.1 us
    pallas_call x1, Pallas kernels, left_partial(): pl.pallas_call(left_kernel, out_shape=(pltpu.VMEM((32, 8, 128), F32), big...  3.45 us

profile of v6, /device:TPU:8, one launch (start us, length us, event | category | flops | bytes accessed | tf_op | source)
XLA Modules:
  0.0 82.3 jit_solution(17468049106061339622)
XLA Ops:
  0.0 3.4 %left_partial.1 = (f32[32,8,128]{2,1,0:T(8,128)S(1)}, bf16[1024,1024]{1,0:T(8,128)(2,1)S(1)}, bf16[1024,1024]{1,0:T(8,128)(2,1)S(1)}, bf16[1024,1024]{1,0:T(8,128)(2,1)S(1)}) custom-call(f32[32,1024]{1,0:T(8,128)} %bitcast.16, bf16[1024,1024]{1,0:T(8,128)(2,1)} %key_hbm.1, bf16[1024,1024]{1,0:T(8,128)(2,1)} %bitcast.15, bf16[1024,1024]{1,0:T(8,128)(2,1)} %hidden_hbm.1), custom_call_target="tpu_custom_call" | custom-call | tf_op jit(solution)/shard_map/left_partial/pallas_call | solution.py:75
  3.5 28.2 %all_to_all.20 = f32[64,4,128]{2,1,0:T(4,128)S(1)} all-to-all(f32[64,4,128]{2,1,0:T(4,128)S(1)} %bitcast.14), channel_id=1, replica_groups=mesh['z2'=2,'z1'=2,'z0'=2,'y2'=2,'y1'=2,'y0'=2,'x'=4,'core'=2] {'y0','z0..., dimensions={0} | all-to-all | bytes 262144 | tf_op jit(solution)/shard_map/all_to_all | solution.py:214
  31.7 15.8 %all_to_all.21 = f32[64,4,128]{2,1,0:T(4,128)S(1)} all-to-all(f32[64,4,128]{2,1,0:T(4,128)S(1)} %bitcast.13), channel_id=1, replica_groups=mesh['z2'=2,'z1'=2,'z0'=2,'y2'=2,'y1'=2,'y0'=2,'x'=4,'core'=2] {'y0','z0..., dimensions={0} | all-to-all | bytes 262144 | tf_op jit(solution)/shard_map/all_to_all | solution.py:214
  47.5 1.4 %right_partial.1 = f32[320,128]{1,0:T(8,128)S(1)} custom-call(f32[32,8,128]{2,1,0:T(8,128)S(1)} %bitcast.11, bf16[1024,1024]{1,0:T(8,128)(2,1)S(1)} %get-tuple-element.12.key, bf16[1024,1024]{1,0:T(8,128)(2,1)S(1)} %get-tuple-element.13.error, bf16[1024,1024]{1,0:T(8,128)(2,1)S(1)} %get-tuple-element.14.hidden), custom_call_target="tpu_custom_call" | custom-call | tf_op jit(solution)/shard_map/right_partial/pallas_call | solution.py:124
  48.9 12.1 %all_to_all.22 = f32[160,2,128]{2,1,0:T(2,128)S(1)} all-to-all(f32[160,2,128]{2,1,0:T(2,128)S(1)} %bitcast.9), channel_id=1, replica_groups=mesh['z2'=2,'z1'=2,'z0'=2,'y2'=2,'y1'=2,'y0'=2,'x'=4,'core'=2] {'x','cor..., dimensions={0} | all-to-all | bytes 327680 | tf_op jit(solution)/shard_map/all_to_all | solution.py:222
  61.0 0.1 right_sum.1
  61.1 19.8 %all_to_all.23.tiles = f32[64,8,128]{2,1,0:T(8,128)S(1)} all-to-all(f32[64,8,128]{2,1,0:T(8,128)S(1)} %get-tuple-element.15), channel_id=1, replica_groups=mesh['z2'=2,'z1'=2,'z0'=2,'y2'=2,'y1'=2,'y0'=2,'x'=4,'core'=2] {'y0','z0..., dimensions={0} | all-to-all | bytes 524288 | tf_op jit(solution)/shard_map/all_to_all | solution.py:224
  80.9 1.4 %finish.1 = f32[32,128]{1,0:T(8,128)} custom-call(f32[64,8,128]{2,1,0:T(8,128)S(1)} %all_to_all.23.tiles, f32[32,128]{1,0:T(8,128)S(1)} %get-tuple-element.16.gram), custom_call_target="tpu_custom_call" | custom-call | tf_op jit(solution)/shard_map/finish/pallas_call | solution.py:203
  (1 shorter events, 0.0 us)

commit v7 on v6

--- a/solution.py
+++ b/solution.py
@@ -132,32 +132,6 @@
     )(*in_vmem(tiles, key, error, hidden))
 
 
-def right_sum_kernel(parts, out, gram):
-    total = parts[:8, :]
-    for k in range(1, 32):
-        total = total + parts[ROWS * k:ROWS * k + 8, :]
-    for k in range(64):
-        out[k] = total
-    for s in range(4):
-        packed = parts[ROWS * s + 8:ROWS * s + ROWS, :]
-        for m in range(1, 8):
-            at = ROWS * (4 * m + s)
-            packed = packed + parts[at + 8:at + ROWS, :]
-        for i in range(4):
-            gram[8 * s + 2 * i:8 * s + 2 * i + 2, :RANK] = packed[:, RANK * i:RANK * i + RANK]
-
-
-def right_sum(parts):
-    return pl.pallas_call(
-        right_sum_kernel,
-        out_shape=(pltpu.VMEM((64, 8, 128), F32), pltpu.VMEM((RANK, 128), F32)),
-        in_specs=[VMEM],
-        out_specs=(VMEM, VMEM),
-        compiler_params=PARAMS,
-        name="right_sum",
-    )(*in_vmem(parts))
-
-
 def along_lanes(tile, j):
     return jnp.broadcast_to(tile[:, j:j + 1], (8, 128))
 
@@ -166,8 +140,8 @@
     return jnp.broadcast_to(tile[j:j + 1, :], (8, 128))
 
 
-def finish_kernel(tiles, gram, out):
-    rows = [jnp.sum(tiles[16 * s:16 * s + 16], 0) for s in (0, 2, 1, 3)]
+def eliminate(gram, rows, out):
+    rows = list(rows)
     rest = [gram[8 * s:8 * s + 8, :] for s in range(4)]
     row = lax.broadcasted_iota(jnp.int32, (8, 128), 0)
     for b in range(4):
@@ -199,7 +173,53 @@
         out[8 * b:8 * b + 8, :] = rows[b] * scale
 
 
-def finish(tiles, gram):
+def right_sum_kernel(parts, out, factor):
+    total = parts[:8, :]
+    for k in range(1, 32):
+        total = total + parts[ROWS * k:ROWS * k + 8, :]
+    for k in range(64):
+        out[k] = total
+    for s in range(4):
+        packed = parts[ROWS * s + 8:ROWS * s + ROWS, :]
+        for m in range(1, 8):
+            at = ROWS * (4 * m + s)
+            packed = packed + parts[at + 8:at + ROWS, :]
+        for i in range(4):
+            factor[8 * s + 2 * i:8 * s + 2 * i + 2, :RANK] = packed[:, RANK * i:RANK * i + RANK]
+
+    @pl.when(lax.axis_index("core") == 0)
+    def _():
+        lane = lax.broadcasted_iota(jnp.int32, (8, 128), 1)
+        row = lax.broadcasted_iota(jnp.int32, (8, 128), 0)
+        eliminate(factor, [jnp.where(lane == row + 8 * s, 1.0, 0.0) for s in range(4)], factor)
+
+
+def right_sum(parts):
+    return pl.pallas_call(
+        right_sum_kernel,
+        out_shape=(pltpu.VMEM((64, 8, 128), F32), pltpu.VMEM((RANK, 128), F32)),
+        in_specs=[VMEM],
+        out_specs=(VMEM, VMEM),
+        compiler_params=PARAMS,
+        name="right_sum",
+    )(*in_vmem(parts))
+
+
+def finish_kernel(tiles, factor, out):
+    rows = [jnp.sum(tiles[16 * s:16 * s + 16], 0) for s in (0, 2, 1, 3)]
+
+    @pl.when(lax.axis_index("core") == 0)
+    def _():
+        out[...] = jnp.dot(
+            factor[:, :RANK], jnp.concatenate(rows, 0), precision=lax.Precision.HIGHEST, preferred_element_type=F32
+        )
+
+    @pl.when(lax.axis_index("core") != 0)
+    def _():
+        eliminate(factor, rows, out)
+
+
+def finish(tiles, factor):
     return pl.pallas_call(
         finish_kernel,
         out_shape=jax.ShapeDtypeStruct((RANK, 128), F32),
@@ -207,7 +227,7 @@
         out_specs=VMEM,
         compiler_params=PARAMS,
         name="finish",
-    )(*in_vmem(tiles, gram))
+    )(*in_vmem(tiles, factor))
 
 
 def halves_over_dp(tiles):
@@ -220,8 +240,8 @@
     tiles = halves_over_dp(left_sum(halves_over_dp(part)))
     part = right_partial(tiles, key, error, hidden).reshape(-1, 2, 128)
     part = lax.all_to_all(part, NEAR, 0, 0, tiled=True).reshape(-1, 128)
-    tiles, gram = right_sum(part)
-    return finish(lax.all_to_all(tiles, STEP_DP, 0, 0, tiled=True), gram).T
+    tiles, factor = right_sum(part)
+    return finish(lax.all_to_all(tiles, STEP_DP, 0, 0, tiled=True), factor).T
 
 
 def solution(mesh):

time: 82.5 us -> 81.9 us (level)
  no operation moved by 1% of the time
where the time goes in v7:
time: 81.9 us; the launch traced here: 81.7 us
  blocking collectives  75.1 us (92%)
  Pallas kernels  6.56 us (8%)
    all_to_all x2, blocking collectives, halves_over_dp(): lax.all_to_all(tiles.reshape(64, 4, 128), STEP_DP, 0, 0, tiled=True)  44 us
    all_to_all x1, blocking collectives, shards(): return finish(lax.all_to_all(tiles, STEP_DP, 0, 0, tiled=True), factor).T  19 us
    all_to_all x1, blocking collectives, shards(): part = lax.all_to_all(part, NEAR, 0, 0, tiled=True).reshape(-1, 128)  12.1 us
    pallas_call x1, Pallas kernels, left_partial(): pl.pallas_call(left_kernel, out_shape=(pltpu.VMEM((32, 8, 128), F32), big...  3.45 us

profile of v7, /device:TPU:8, one launch (start us, length us, event | category | flops | bytes accessed | tf_op | source)
XLA Modules:
  0.0 81.7 jit_solution(7500440577888226746)
XLA Ops:
  0.0 3.4 %left_partial.1 = (f32[32,8,128]{2,1,0:T(8,128)S(1)}, bf16[1024,1024]{1,0:T(8,128)(2,1)S(1)}, bf16[1024,1024]{1,0:T(8,128)(2,1)S(1)}, bf16[1024,1024]{1,0:T(8,128)(2,1)S(1)}) custom-call(f32[32,1024]{1,0:T(8,128)} %bitcast.16, bf16[1024,1024]{1,0:T(8,128)(2,1)} %key_hbm.1, bf16[1024,1024]{1,0:T(8,128)(2,1)} %bitcast.15, bf16[1024,1024]{1,0:T(8,128)(2,1)} %hidden_hbm.1), custom_call_target="tpu_custom_call" | custom-call | tf_op jit(solution)/shard_map/left_partial/pallas_call | solution.py:75
  3.5 28.2 %all_to_all.20 = f32[64,4,128]{2,1,0:T(4,128)S(1)} all-to-all(f32[64,4,128]{2,1,0:T(4,128)S(1)} %bitcast.14), channel_id=1, replica_groups=mesh['z2'=2,'z1'=2,'z0'=2,'y2'=2,'y1'=2,'y0'=2,'x'=4,'core'=2] {'y0','z0..., dimensions={0} | all-to-all | bytes 262144 | tf_op jit(solution)/shard_map/all_to_all | solution.py:234
  31.7 15.8 %all_to_all.21 = f32[64,4,128]{2,1,0:T(4,128)S(1)} all-to-all(f32[64,4,128]{2,1,0:T(4,128)S(1)} %bitcast.13), channel_id=1, replica_groups=mesh['z2'=2,'z1'=2,'z0'=2,'y2'=2,'y1'=2,'y0'=2,'x'=4,'core'=2] {'y0','z0..., dimensions={0} | all-to-all | bytes 262144 | tf_op jit(solution)/shard_map/all_to_all | solution.py:234
  47.5 1.4 %right_partial.1 = f32[320,128]{1,0:T(8,128)S(1)} custom-call(f32[32,8,128]{2,1,0:T(8,128)S(1)} %bitcast.11, bf16[1024,1024]{1,0:T(8,128)(2,1)S(1)} %get-tuple-element.12.key, bf16[1024,1024]{1,0:T(8,128)(2,1)S(1)} %get-tuple-element.13.error, bf16[1024,1024]{1,0:T(8,128)(2,1)S(1)} %get-tuple-element.14.hidden), custom_call_target="tpu_custom_call" | custom-call | tf_op jit(solution)/shard_map/right_partial/pallas_call | solution.py:124
  48.9 12.1 %all_to_all.22 = f32[160,2,128]{2,1,0:T(2,128)S(1)} all-to-all(f32[160,2,128]{2,1,0:T(2,128)S(1)} %bitcast.9), channel_id=1, replica_groups=mesh['z2'=2,'z1'=2,'z0'=2,'y2'=2,'y1'=2,'y0'=2,'x'=4,'core'=2] {'x','cor..., dimensions={0} | all-to-all | bytes 327680 | tf_op jit(solution)/shard_map/all_to_all | solution.py:242
  61.0 0.9 %right_sum.1 = (f32[64,8,128]{2,1,0:T(8,128)S(1)}, f32[32,128]{1,0:T(8,128)S(1)}) custom-call(f32[320,128]{1,0:T(8,128)S(1)} %bitcast.10), custom_call_target="tpu_custom_call" | custom-call | tf_op jit(solution)/shard_map/right_sum/pallas_call | solution.py:198
  61.9 19.0 %all_to_all.23.tiles = f32[64,8,128]{2,1,0:T(8,128)S(1)} all-to-all(f32[64,8,128]{2,1,0:T(8,128)S(1)} %get-tuple-element.15), channel_id=1, replica_groups=mesh['z2'=2,'z1'=2,'z0'=2,'y2'=2,'y1'=2,'y0'=2,'x'=4,'core'=2] {'y0','z0..., dimensions={0} | all-to-all | bytes 524288 | tf_op jit(solution)/shard_map/all_to_all | solution.py:244
  80.9 0.8 finish.1
  (1 shorter events, 0.0 us)

commit v8 on v7

--- a/solution.py
+++ b/solution.py
@@ -7,7 +7,7 @@
 
 DP = ("z2", "z1", "z0", "y2", "y1", "y0")
 MP = ("x", "core")
-STEP_DP = ("y0", "z0", "y1", "z1", "y2", "z2")
+STEP_DP = ("y0", "z0", "y1", "z1", "z2", "y2")
 NEAR = ("x", "core", "z0", "y0")
 
 F32, BF16 = jnp.float32, jnp.bfloat16

time: 81.9 us -> 81.7 us (level)
  no operation moved by 1% of the time
where the time goes in v8:
time: 81.7 us; the launch traced here: 81.5 us
  blocking collectives  74.9 us (92%)
  Pallas kernels  6.56 us (8%)
    all_to_all x2, blocking collectives, halves_over_dp(): lax.all_to_all(tiles.reshape(64, 4, 128), STEP_DP, 0, 0, tiled=True)  44 us
    all_to_all x1, blocking collectives, shards(): return finish(lax.all_to_all(tiles, STEP_DP, 0, 0, tiled=True), factor).T  18.8 us
    all_to_all x1, blocking collectives, shards(): part = lax.all_to_all(part, NEAR, 0, 0, tiled=True).reshape(-1, 128)  12.1 us
    pallas_call x1, Pallas kernels, left_partial(): pl.pallas_call(left_kernel, out_shape=(pltpu.VMEM((32, 8, 128), F32), big...  3.45 us

profile of v8, /device:TPU:8, one launch (start us, length us, event | category | flops | bytes accessed | tf_op | source)
XLA Modules:
  0.0 81.5 jit_solution(16230324356402068291)
XLA Ops:
  0.0 3.4 %left_partial.1 = (f32[32,8,128]{2,1,0:T(8,128)S(1)}, bf16[1024,1024]{1,0:T(8,128)(2,1)S(1)}, bf16[1024,1024]{1,0:T(8,128)(2,1)S(1)}, bf16[1024,1024]{1,0:T(8,128)(2,1)S(1)}) custom-call(f32[32,1024]{1,0:T(8,128)} %bitcast.16, bf16[1024,1024]{1,0:T(8,128)(2,1)} %key_hbm.1, bf16[1024,1024]{1,0:T(8,128)(2,1)} %bitcast.15, bf16[1024,1024]{1,0:T(8,128)(2,1)} %hidden_hbm.1), custom_call_target="tpu_custom_call" | custom-call | tf_op jit(solution)/shard_map/left_partial/pallas_call | solution.py:75
  3.5 28.1 %all_to_all.20 = f32[64,4,128]{2,1,0:T(4,128)S(1)} all-to-all(f32[64,4,128]{2,1,0:T(4,128)S(1)} %bitcast.14), channel_id=1, replica_groups=mesh['z2'=2,'z1'=2,'z0'=2,'y2'=2,'y1'=2,'y0'=2,'x'=4,'core'=2] {'y0','z0..., dimensions={0} | all-to-all | bytes 262144 | tf_op jit(solution)/shard_map/all_to_all | solution.py:234
  31.6 15.9 %all_to_all.21 = f32[64,4,128]{2,1,0:T(4,128)S(1)} all-to-all(f32[64,4,128]{2,1,0:T(4,128)S(1)} %bitcast.13), channel_id=1, replica_groups=mesh['z2'=2,'z1'=2,'z0'=2,'y2'=2,'y1'=2,'y0'=2,'x'=4,'core'=2] {'y0','z0..., dimensions={0} | all-to-all | bytes 262144 | tf_op jit(solution)/shard_map/all_to_all | solution.py:234
  47.5 1.4 %right_partial.1 = f32[320,128]{1,0:T(8,128)S(1)} custom-call(f32[32,8,128]{2,1,0:T(8,128)S(1)} %bitcast.11, bf16[1024,1024]{1,0:T(8,128)(2,1)S(1)} %get-tuple-element.12.key, bf16[1024,1024]{1,0:T(8,128)(2,1)S(1)} %get-tuple-element.13.error, bf16[1024,1024]{1,0:T(8,128)(2,1)S(1)} %get-tuple-element.14.hidden), custom_call_target="tpu_custom_call" | custom-call | tf_op jit(solution)/shard_map/right_partial/pallas_call | solution.py:124
  48.9 12.1 %all_to_all.22 = f32[160,2,128]{2,1,0:T(2,128)S(1)} all-to-all(f32[160,2,128]{2,1,0:T(2,128)S(1)} %bitcast.9), channel_id=1, replica_groups=mesh['z2'=2,'z1'=2,'z0'=2,'y2'=2,'y1'=2,'y0'=2,'x'=4,'core'=2] {'x','cor..., dimensions={0} | all-to-all | bytes 327680 | tf_op jit(solution)/shard_map/all_to_all | solution.py:242
  61.0 0.9 %right_sum.1 = (f32[64,8,128]{2,1,0:T(8,128)S(1)}, f32[32,128]{1,0:T(8,128)S(1)}) custom-call(f32[320,128]{1,0:T(8,128)S(1)} %bitcast.10), custom_call_target="tpu_custom_call" | custom-call | tf_op jit(solution)/shard_map/right_sum/pallas_call | solution.py:198
  61.9 18.8 %all_to_all.23.tiles = f32[64,8,128]{2,1,0:T(8,128)S(1)} all-to-all(f32[64,8,128]{2,1,0:T(8,128)S(1)} %get-tuple-element.15), channel_id=1, replica_groups=mesh['z2'=2,'z1'=2,'z0'=2,'y2'=2,'y1'=2,'y0'=2,'x'=4,'core'=2] {'y0','z0..., dimensions={0} | all-to-all | bytes 524288 | tf_op jit(solution)/shard_map/all_to_all | solution.py:244
  80.7 0.8 finish.1
  (1 shorter events, 0.0 us)

commit v9 on v7

--- a/solution.py
+++ b/solution.py
@@ -68,6 +68,10 @@
     for k in range(32):
         out[k] = total[8 * (k % 4):8 * (k % 4) + 8, 128 * (k // 4):128 * (k // 4) + 128]
 
+    @pl.when(lax.axis_index("core") == 0)
+    def _():
+        hidden[...] = jnp.transpose(hidden[...])
+
 
 def left_partial(q_t, key, error, hidden):
     big = pltpu.VMEM((WIDTH, WIDTH), BF16)
@@ -101,7 +105,17 @@
     )(*in_vmem(parts))
 
 
-def right_kernel(tiles, key, error, hidden, out, gram):
+def right_kernel(*refs):
+    @pl.when(lax.axis_index("core") == 0)
+    def _():
+        right_factor(NN, *refs)
+
+    @pl.when(lax.axis_index("core") != 0)
+    def _():
+        right_factor(NT, *refs)
+
+
+def right_factor(dims, tiles, key, error, hidden, out, gram):
     columns = [
         jnp.concatenate([tiles[4 * b + a] for a in range(4)], 0) for b in range(8)
     ]
@@ -111,7 +125,7 @@
     quarter = 2 * lax.axis_index("z0") + lax.axis_index("y0")
     own = gram[pl.ds(pl.multiple_of(8 * quarter, 8), 8), :]
     packed = jnp.concatenate([own[2 * i:2 * i + 2] for i in range(4)], 1)
-    inner = pieces(fold(dot(p3, hidden[...], NT)))
+    inner = pieces(fold(dot(p3, hidden[...], dims)))
     total = (fold(dot(p3, error[...], NN)) + fold(dot(inner, key[...], NN))) * (1 / 64)
     for m in range(8):
         for s in range(4):

time: 81.9 us -> 82.3 us (level)
  no operation moved by 1% of the time
where the time goes in v9:
time: 82.3 us; the launch traced here: 82.1 us
  blocking collectives  75 us (91%)
  Pallas kernels  7.02 us (9%)
    all_to_all x2, blocking collectives, halves_over_dp(): lax.all_to_all(tiles.reshape(64, 4, 128), STEP_DP, 0, 0, tiled=True)  44 us
    all_to_all x1, blocking collectives, shards(): return finish(lax.all_to_all(tiles, STEP_DP, 0, 0, tiled=True), factor).T  19 us
    all_to_all x1, blocking collectives, shards(): part = lax.all_to_all(part, NEAR, 0, 0, tiled=True).reshape(-1, 128)  12.1 us
    pallas_call x1, Pallas kernels, left_partial(): pl.pallas_call(left_kernel, out_shape=(pltpu.VMEM((32, 8, 128), F32), big...  4.11 us

profile of v9, /device:TPU:8, one launch (start us, length us, event | category | flops | bytes accessed | tf_op | source)
XLA Modules:
  0.0 82.1 jit_solution(4443813991068266067)
XLA Ops:
  0.0 4.1 %left_partial.1 = (f32[32,8,128]{2,1,0:T(8,128)S(1)}, bf16[1024,1024]{1,0:T(8,128)(2,1)S(1)}, bf16[1024,1024]{1,0:T(8,128)(2,1)S(1)}, bf16[1024,1024]{1,0:T(8,128)(2,1)S(1)}) custom-call(f32[32,1024]{1,0:T(8,128)} %bitcast.16, bf16[1024,1024]{1,0:T(8,128)(2,1)} %key_hbm.1, bf16[1024,1024]{1,0:T(8,128)(2,1)} %bitcast.15, bf16[1024,1024]{1,0:T(8,128)(2,1)} %hidden_hbm.1), custom_call_target="tpu_custom_call" | custom-call | tf_op jit(solution)/shard_map/left_partial/pallas_call | solution.py:79
  4.1 28.1 %all_to_all.20 = f32[64,4,128]{2,1,0:T(4,128)S(1)} all-to-all(f32[64,4,128]{2,1,0:T(4,128)S(1)} %bitcast.14), channel_id=1, replica_groups=mesh['z2'=2,'z1'=2,'z0'=2,'y2'=2,'y1'=2,'y0'=2,'x'=4,'core'=2] {'y0','z0..., dimensions={0} | all-to-all | bytes 262144 | tf_op jit(solution)/shard_map/all_to_all | solution.py:248
  32.2 15.9 %all_to_all.21 = f32[64,4,128]{2,1,0:T(4,128)S(1)} all-to-all(f32[64,4,128]{2,1,0:T(4,128)S(1)} %bitcast.13), channel_id=1, replica_groups=mesh['z2'=2,'z1'=2,'z0'=2,'y2'=2,'y1'=2,'y0'=2,'x'=4,'core'=2] {'y0','z0..., dimensions={0} | all-to-all | bytes 262144 | tf_op jit(solution)/shard_map/all_to_all | solution.py:248
  48.1 1.2 %right_partial.1 = f32[320,128]{1,0:T(8,128)S(1)} custom-call(f32[32,8,128]{2,1,0:T(8,128)S(1)} %bitcast.11, bf16[1024,1024]{1,0:T(8,128)(2,1)S(1)} %get-tuple-element.12.refs_1_, bf16[1024,1024]{1,0:T(8,128)(2,1)S(1)} %get-tuple-element.13.refs_2_, bf16[1024,1024]{1,0:T(8,128)(2,1)S(1)} %get-tuple-element.14.refs_3_), custom_call_target="tpu_custom_call" | custom-call | tf_op jit(solution)/shard_map/right_partial/pallas_call | solution.py:138
  49.3 12.1 %all_to_all.22 = f32[160,2,128]{2,1,0:T(2,128)S(1)} all-to-all(f32[160,2,128]{2,1,0:T(2,128)S(1)} %bitcast.9), channel_id=1, replica_groups=mesh['z2'=2,'z1'=2,'z0'=2,'y2'=2,'y1'=2,'y0'=2,'x'=4,'core'=2] {'x','cor..., dimensions={0} | all-to-all | bytes 327680 | tf_op jit(solution)/shard_map/all_to_all | solution.py:256
  61.4 0.9 %right_sum.1 = (f32[64,8,128]{2,1,0:T(8,128)S(1)}, f32[32,128]{1,0:T(8,128)S(1)}) custom-call(f32[320,128]{1,0:T(8,128)S(1)} %bitcast.10), custom_call_target="tpu_custom_call" | custom-call | tf_op jit(solution)/shard_map/right_sum/pallas_call | solution.py:212
  62.4 19.0 %all_to_all.23.tiles = f32[64,8,128]{2,1,0:T(8,128)S(1)} all-to-all(f32[64,8,128]{2,1,0:T(8,128)S(1)} %get-tuple-element.15), channel_id=1, replica_groups=mesh['z2'=2,'z1'=2,'z0'=2,'y2'=2,'y1'=2,'y0'=2,'x'=4,'core'=2] {'y0','z0..., dimensions={0} | all-to-all | bytes 524288 | tf_op jit(solution)/shard_map/all_to_all | solution.py:258
  81.3 0.8 finish.1
  (1 shorter events, 0.0 us)

commit v10 on v7

--- a/solution.py
+++ b/solution.py
@@ -173,24 +173,28 @@
         out[8 * b:8 * b + 8, :] = rows[b] * scale
 
 
+def collect_gram(parts, gram):
+    for s in range(4):
+        packed = parts[ROWS * s + 8:ROWS * s + ROWS, :]
+        for m in range(1, 8):
+            at = ROWS * (4 * m + s)
+            packed = packed + parts[at + 8:at + ROWS, :]
+        for i in range(4):
+            gram[8 * s + 2 * i:8 * s + 2 * i + 2, :RANK] = packed[:, RANK * i:RANK * i + RANK]
+
+
 def right_sum_kernel(parts, out, factor):
     total = parts[:8, :]
     for k in range(1, 32):
         total = total + parts[ROWS * k:ROWS * k + 8, :]
     for k in range(64):
         out[k] = total
-    for s in range(4):
-        packed = parts[ROWS * s + 8:ROWS * s + ROWS, :]
-        for m in range(1, 8):
-            at = ROWS * (4 * m + s)
-            packed = packed + parts[at + 8:at + ROWS, :]
-        for i in range(4):
-            factor[8 * s + 2 * i:8 * s + 2 * i + 2, :RANK] = packed[:, RANK * i:RANK * i + RANK]
 
     @pl.when(lax.axis_index("core") == 0)
     def _():
         lane = lax.broadcasted_iota(jnp.int32, (8, 128), 1)
         row = lax.broadcasted_iota(jnp.int32, (8, 128), 0)
+        collect_gram(parts, factor)
         eliminate(factor, [jnp.where(lane == row + 8 * s, 1.0, 0.0) for s in range(4)], factor)
 
 
@@ -205,7 +209,7 @@
     )(*in_vmem(parts))
 
 
-def finish_kernel(tiles, factor, out):
+def finish_kernel(tiles, factor, parts, out, gram):
     rows = [jnp.sum(tiles[16 * s:16 * s + 16], 0) for s in (0, 2, 1, 3)]
 
     @pl.when(lax.axis_index("core") == 0)
@@ -216,18 +220,20 @@
 
     @pl.when(lax.axis_index("core") != 0)
     def _():
-        eliminate(factor, rows, out)
-
-
-def finish(tiles, factor):
+        collect_gram(parts, gram)
+        eliminate(gram, rows, out)
+
+
+def finish(tiles, factor, parts):
     return pl.pallas_call(
         finish_kernel,
         out_shape=jax.ShapeDtypeStruct((RANK, 128), F32),
-        in_specs=[VMEM, VMEM],
+        in_specs=[VMEM] * 3,
         out_specs=VMEM,
+        scratch_shapes=[pltpu.VMEM((RANK, 128), F32)],
         compiler_params=PARAMS,
         name="finish",
-    )(*in_vmem(tiles, factor))
+    )(*in_vmem(tiles, factor, parts))
 
 
 def halves_over_dp(tiles):
@@ -241,7 +247,7 @@
     part = right_partial(tiles, key, error, hidden).reshape(-1, 2, 128)
     part = lax.all_to_all(part, NEAR, 0, 0, tiled=True).reshape(-1, 128)
     tiles, factor = right_sum(part)
-    return finish(lax.all_to_all(tiles, STEP_DP, 0, 0, tiled=True), factor).T
+    return finish(lax.all_to_all(tiles, STEP_DP, 0, 0, tiled=True), factor, part).T
 
 
 def solution(mesh):

time: 81.9 us -> 82 us (level)
  no operation moved by 1% of the time
where the time goes in v10:
time: 82 us; the launch traced here: 81.7 us
  blocking collectives  75.1 us (92%)
  Pallas kernels  6.64 us (8%)
    all_to_all x2, blocking collectives, halves_over_dp(): lax.all_to_all(tiles.reshape(64, 4, 128), STEP_DP, 0, 0, tiled=True)  44 us
    all_to_all x1, blocking collectives, shards(): lax.all_to_all(tiles, STEP_DP, 0, 0, tiled=True)  19 us
    all_to_all x1, blocking collectives, shards(): part = lax.all_to_all(part, NEAR, 0, 0, tiled=True).reshape(-1, 128)  12.1 us
    pallas_call x1, Pallas kernels, left_partial(): pl.pallas_call(left_kernel, out_shape=(pltpu.VMEM((32, 8, 128), F32), big...  3.45 us

profile of v10, /device:TPU:8, one launch (start us, length us, event | category | flops | bytes accessed | tf_op | source)
XLA Modules:
  0.0 81.7 jit_solution(10903635715513968724)
XLA Ops:
  0.0 3.4 %left_partial.1 = (f32[32,8,128]{2,1,0:T(8,128)S(1)}, bf16[1024,1024]{1,0:T(8,128)(2,1)S(1)}, bf16[1024,1024]{1,0:T(8,128)(2,1)S(1)}, bf16[1024,1024]{1,0:T(8,128)(2,1)S(1)}) custom-call(f32[32,1024]{1,0:T(8,128)} %bitcast.17, bf16[1024,1024]{1,0:T(8,128)(2,1)} %key_hbm.1, bf16[1024,1024]{1,0:T(8,128)(2,1)} %bitcast.16, bf16[1024,1024]{1,0:T(8,128)(2,1)} %hidden_hbm.1), custom_call_target="tpu_custom_call" | custom-call | tf_op jit(solution)/shard_map/left_partial/pallas_call | solution.py:75
  3.5 28.2 %all_to_all.20 = f32[64,4,128]{2,1,0:T(4,128)S(1)} all-to-all(f32[64,4,128]{2,1,0:T(4,128)S(1)} %bitcast.15), channel_id=1, replica_groups=mesh['z2'=2,'z1'=2,'z0'=2,'y2'=2,'y1'=2,'y0'=2,'x'=4,'core'=2] {'y0','z0..., dimensions={0} | all-to-all | bytes 262144 | tf_op jit(solution)/shard_map/all_to_all | solution.py:240
  31.7 15.8 %all_to_all.21 = f32[64,4,128]{2,1,0:T(4,128)S(1)} all-to-all(f32[64,4,128]{2,1,0:T(4,128)S(1)} %bitcast.14), channel_id=1, replica_groups=mesh['z2'=2,'z1'=2,'z0'=2,'y2'=2,'y1'=2,'y0'=2,'x'=4,'core'=2] {'y0','z0..., dimensions={0} | all-to-all | bytes 262144 | tf_op jit(solution)/shard_map/all_to_all | solution.py:240
  47.5 1.4 %right_partial.1 = f32[320,128]{1,0:T(8,128)S(1)} custom-call(f32[32,8,128]{2,1,0:T(8,128)S(1)} %bitcast.12, bf16[1024,1024]{1,0:T(8,128)(2,1)S(1)} %get-tuple-element.12.key, bf16[1024,1024]{1,0:T(8,128)(2,1)S(1)} %get-tuple-element.13.error, bf16[1024,1024]{1,0:T(8,128)(2,1)S(1)} %get-tuple-element.14.hidden), custom_call_target="tpu_custom_call" | custom-call | tf_op jit(solution)/shard_map/right_partial/pallas_call | solution.py:124
  48.9 12.1 %all_to_all.22 = f32[160,2,128]{2,1,0:T(2,128)S(1)} all-to-all(f32[160,2,128]{2,1,0:T(2,128)S(1)} %bitcast.11), channel_id=1, replica_groups=mesh['z2'=2,'z1'=2,'z0'=2,'y2'=2,'y1'=2,'y0'=2,'x'=4,'core'=2] {'x','cor..., dimensions={0} | all-to-all | bytes 327680 | tf_op jit(solution)/shard_map/all_to_all | solution.py:248
  61.0 1.0 %right_sum.1 = (f32[64,8,128]{2,1,0:T(8,128)S(1)}, f32[32,128]{1,0:T(8,128)S(1)}) custom-call(f32[320,128]{1,0:T(8,128)S(1)} %bitcast.9), custom_call_target="tpu_custom_call" | custom-call | tf_op jit(solution)/shard_map/right_sum/pallas_call | solution.py:202
  62.0 19.0 %all_to_all.23.tiles = f32[64,8,128]{2,1,0:T(8,128)S(1)} all-to-all(f32[64,8,128]{2,1,0:T(8,128)S(1)} %get-tuple-element.15), channel_id=1, replica_groups=mesh['z2'=2,'z1'=2,'z0'=2,'y2'=2,'y1'=2,'y0'=2,'x'=4,'core'=2] {'y0','z0..., dimensions={0} | all-to-all | bytes 524288 | tf_op jit(solution)/shard_map/all_to_all | solution.py:250
  81.0 0.8 finish.1
  (1 shorter events, 0.0 us)
